TPU v7x, 256 devices: a whole 4x4x8 slice. The times are simulated.
256 devices in a mesh: gx: 16 (over z, core), gy: 16 (over y, x).
Axes of the slice: x: 4, y: 4, z: 8, core: 2. Of those that a mesh axis runs over, the one named last changes fastest.
Arguments:
- tokens: bfloat16 [128, 8192], P(None, 'gx'), may hold values from -150 to 150
- norm_gain: float32 [8192], P('gx'), may hold values from 0.25 to 1.75
- w_project: bfloat16 [8192, 4, 8192], P('gx', None, 'gy'), may hold values from -0.0625 to 0.0625
- w_output: bfloat16 [8192, 8192], P('gy', 'gx'), may hold values from -0.0625 to 0.0625
- decay: float32 [32], P('gy'), may hold values from 0.5 to 0.99
- state: float32 [128, 32, 256, 256], P('gx', 'gy'), may hold values from -3 to 3
Outputs:
- mixed: bfloat16 [128, 8192], P(None, 'gx')
- new_state: float32 [128, 32, 256, 256], P('gx', 'gy')
All inputs are finite; a program needn't handle non-finite values.
Results may differ from a plain program's by a relative error of at most 0.009.
Values may be sent and summed in bfloat16 or wider, within the bound.
No kernel may reach another device: no remote copies, remote signals or barrier semaphores. Data moves between devices by JAX's collectives and lax.ppermute only.
A program may use at most 64 MiB of HBM per device.

v0:
```python
import jax
import jax.numpy as jnp
from jax import lax
from jax.sharding import PartitionSpec as P

HS = 256
D = 8192


def local(tokens, norm_gain, w_project, w_output, decay, state):
    all_rows = tokens.shape[0]
    own_rows = all_rows // lax.axis_size("gx")
    first_row = lax.axis_index("gx") * own_rows
    tokens_f = tokens.astype(jnp.float32)
    squares = jnp.sum(tokens_f * tokens_f, axis=1)
    totals = lax.psum(squares, "gx")
    inverse_rms = lax.rsqrt(totals / D + 1e-06)
    scaled_in = (tokens_f * norm_gain).astype(jnp.bfloat16)
    flat_weights = w_project.reshape(w_project.shape[0], -1)
    partial_all = jnp.dot(scaled_in, flat_weights, preferred_element_type=jnp.float32)
    summed_all = lax.psum(partial_all.astype(jnp.bfloat16), "gx").astype(jnp.float32)
    summed = lax.dynamic_slice_in_dim(summed_all, first_row, own_rows, 0)
    own_scale = lax.dynamic_slice_in_dim(inverse_rms, first_row, own_rows, 0)
    heads_here = state.shape[1]
    projected = (summed * own_scale[:, None]).reshape(own_rows, 4, heads_here, HS)
    query = projected[:, 0]
    keys_scaled = projected[:, 1] * HS ** (-0.5)
    values = projected[:, 2]
    gates = projected[:, 3].reshape(own_rows, heads_here * HS)
    new_state = (
        decay[None, :, None, None] * state + keys_scaled[:, :, :, None] * values[:, :, None, :]
    )
    readout = jnp.einsum("shk,shkv->shv", query, new_state, precision=lax.Precision.HIGHEST)
    centre = jnp.mean(readout, axis=2, keepdims=True)
    spread = jnp.mean((readout - centre) ** 2, axis=2, keepdims=True)
    normed = (readout - centre) * lax.rsqrt(spread + 1e-05)
    gated = (jax.nn.silu(gates) * normed.reshape(own_rows, heads_here * HS)).astype(jnp.bfloat16)
    head_terms = jnp.dot(
        lax.all_gather(gated, "gx", axis=0, tiled=True),
        w_output,
        preferred_element_type=jnp.float32,
    )
    head_total = lax.psum(head_terms.astype(jnp.bfloat16), "gy").astype(jnp.float32)
    mixed = (tokens_f + head_total).astype(jnp.bfloat16)
    return (mixed, new_state)


def solution(mesh):
    placed = (
        P(None, "gx"),
        P("gx"),
        P("gx", None, "gy"),
        P("gy", "gx"),
        P("gy"),
        P("gx", "gy", None, None),
    )
    return jax.shard_map(
        local,
        mesh=mesh,
        in_specs=placed,
        out_specs=(P(None, "gx"), P("gx", "gy", None, None)),
        check_vma=False,
    )
```

profile of v0, /device:TPU:1, one launch (start us, length us, event | category | flops | bytes accessed | tf_op | source)
XLA Modules:
  0.0 248.1 jit_solution(1820187456763777886)
XLA Ops:
  7.2 0.0 copy-start
  7.2 0.0 copy-start.2
  7.2 0.0 copy-start.3
  7.2 0.0 copy-start.4
  7.2 0.0 all-reduce.3.cloned.1.call-start
  7.3 2.3 copy.14
  9.5 0.0 copy-done.2
  9.6 0.0 copy-done.3
  9.6 1.2 convolution_convert_fusion
  10.8 0.0 all-reduce.3.cloned.1.call-update
  10.8 0.0 all-reduce.5.cloned.1.call-start
  10.9 0.1 fusion.1
  11.0 27.4 %psum.22 = f32[128]{0:T(128)S(1)} all-reduce(f32[128]{0:T(128)S(1)} %fusion.1), channel_id=1, replica_groups=mesh['gx'=16,'gy'=16] {'gx'}, use_global_device_ids=true, to_apply=%region_2.0 | all-reduce | flops 128 | bytes 1024 | tf_op jit(solution)/shard_map/psum | solution.py:16
  38.4 0.1 dynamic_slice.7
  38.5 85.9 %all-reduce.3.cloned.1.call-done = bf16[128,2048]{1,0:T(8,128)(2,1)} async-done(((bf16[128,2048]{1,0:T(8,128)(2,1)}), bf16[128,2048]{1,0:T(8,128)(2,1)}) %all-reduce.3.cloned.1.call-update) | async-done | bytes 524304 | tf_op jit(solution)/shard_map/psum | solution.py:21
  124.4 0.8 convert_multiply_fusion.2
  125.3 0.0 copy-done.4
  125.3 2.6 %multiply_add_fusion = f32[8,2,256,256]{3,2,1,0:T(8,128)S(1)} fusion(f32[8,2,256,256]{3,2,1,0:T(8,128)} %param.11, f32[8,2,256]{2,1,0:T(2,128)S(1)} %copy.11, f32[8,2,256]{2,1,0:T(2,128)S(1)} %copy.10, f32[2]{0:T(128)S(1)} %copy-done.4), kind=kLoop, calls=%fused_computation | loop fusion | flops 3145728 | bytes 8421384 | tf_op jit(solution)/shard_map/add | solution.py:31
  127.9 0.0 copy-start.1
  127.9 2.0 copy-done.1
  129.9 2.1 fusion.6
  132.0 0.1 bitcast_reduce_fusion
  132.1 0.2 multiply_reduce_fusion
  132.3 0.1 fusion.8
  132.4 15.6 %all_gather.3 = bf16[128,512]{1,0:T(8,128)(2,1)S(1)} all-gather(bf16[8,512]{1,0:T(8,128)(2,1)S(1)} %multiply_convert_fusion), channel_id=1, replica_groups=mesh['gx'=16,'gy'=16] {'gx'}, dimensions={0}, use_global_device_ids=true | all-gather | bytes 139264 | tf_op jit(solution)/shard_map/all_gather | solution.py:39
  148.0 0.0 copy-done
  148.0 0.9 convolution_convert_fusion.1
  148.9 0.0 all-reduce.5.cloned.1.call-update
  148.9 90.7 %all-reduce.5.cloned.1.call-done = bf16[128,512]{1,0:T(8,128)(2,1)} async-done(((bf16[128,512]{1,0:T(8,128)(2,1)}), bf16[128,512]{1,0:T(8,128)(2,1)}) %all-reduce.5.cloned.1.call-update) | async-done | bytes 131088 | tf_op jit(solution)/shard_map/psum | solution.py:43
  239.7 1.6 fusion.2
  (7 shorter events, 0.1 us)
Async XLA Ops:
  7.2 140.8 %copy-start = (bf16[512,512]{1,0:T(8,128)(2,1)S(1)}, bf16[512,512]{1,0:T(8,128)(2,1)}, u32[]{:S(2)}) copy-start(bf16[512,512]{1,0:T(8,128)(2,1)} %param.9) | copy-start | bytes 1572868
  7.2 2.4 copy-start.2
  7.2 2.4 copy-start.3
  7.2 118.1 %copy-start.4 = (f32[2]{0:T(128)S(1)}, f32[2]{0:T(128)}, u32[]{:S(2)}) copy-start(f32[2]{0:T(128)} %param.10) | copy-start | bytes 28
  7.2 117.2 %all-reduce.3.cloned.1.call-start = ((), (), s32[]{:S(2)}) async-start(), calls=%async_computation | async-start | bytes 1048576 | tf_op jit(solution)/shard_map/psum | solution.py:21
  10.8 228.8 %all-reduce.5.cloned.1.call-start = ((), (), s32[]{:S(2)}) async-start(), calls=%async_computation.1 | async-start | bytes 262144 | tf_op jit(solution)/shard_map/psum | solution.py:43
  127.9 2.0 copy-start.1
Sparse Core Ops, SparseCore 0:
  11.0 113.4 all-reduce.2
  149.0 90.5 all-reduce.4
where the time goes:
time: 249 us; the launch traced here: 248 us
  waiting for transfers between devices  177 us (71%)
  blocking collectives  43 us (17%)
  between operations  14.2 us (6%)
  other arithmetic  5.53 us (2%)
  local copies, waits for them, and re-layouts  4.41 us (2%)
  matrix products  4.22 us (2%)
    psum x1, waiting for transfers between devices, local(): lax.psum(head_terms.astype(jnp.bfloat16), 'gy').astype(jnp.float32)  90.7 us
    psum x1, waiting for transfers between devices, local(): lax.psum(partial_all.astype(jnp.bfloat16), 'gx').astype(jnp.float32)  85.9 us
    psum x1, blocking collectives, local(): totals = lax.psum(squares, 'gx')  27.4 us
    all_gather x1, blocking collectives, local(): lax.all_gather(gated, 'gx', axis=0, tiled=True)  15.6 us
  transfers between devices with their start and end apart: 2, of which 2 were waited for; matrix products, arithmetic and copies ran while one was open for 0% of the time, Pallas kernels for 0%

commit v1 on v0

v1 whole, which is shorter than its diff:
```python
import jax
import jax.numpy as jnp
from jax import lax
from jax.experimental import pallas as pl
from jax.experimental.pallas import tpu as pltpu
from jax.sharding import PartitionSpec as P

HS = 256
D = 8192
LANES = 128


def state_kernel(decay_ref, parts_ref, state_ref, new_ref, gated_ref, cols_ref):
    pieces, rows, _ = parts_ref.shape
    heads = state_ref.shape[1]
    width = heads * HS
    summed = parts_ref[0].astype(jnp.float32)
    for z in range(1, pieces):
        summed += parts_ref[z].astype(jnp.float32)
    squares = summed[:, 4 * width : 4 * width + 1] + summed[:, 4 * width + 1 : 4 * width + 2]
    scale = lax.rsqrt(squares / D + 1e-06)
    projected = summed[:, : 4 * width] * scale
    queries = projected[:, :width]
    keys = projected[:, width : 2 * width] * HS ** (-0.5)
    values = projected[:, 2 * width : 3 * width]
    gates = projected[:, 3 * width : 4 * width]
    cols_ref[0] = queries.T
    cols_ref[1] = keys.T
    readouts = []
    for h in range(heads):
        decay = decay_ref[h]
        per_head = []
        for s in range(rows):
            key_col = cols_ref[1, h * HS : (h + 1) * HS, s : s + 1]
            query_col = cols_ref[0, h * HS : (h + 1) * HS, s : s + 1]
            value_row = values[s : s + 1, h * HS : (h + 1) * HS]
            updated = decay * state_ref[s, h] + key_col * value_row
            new_ref[s, h] = updated
            per_head.append(jnp.sum(query_col * updated, axis=0, keepdims=True))
        readout = jnp.concatenate(per_head, axis=0)
        centre = jnp.mean(readout, axis=1, keepdims=True)
        spread = jnp.mean((readout - centre) ** 2, axis=1, keepdims=True)
        readouts.append((readout - centre) * lax.rsqrt(spread + 1e-05))
    normed = jnp.concatenate(readouts, axis=1)
    gated = gates / (1.0 + jnp.exp(-gates)) * normed
    gated_ref[...] = gated.astype(jnp.bfloat16)


def local(tokens, norm_gain, w_project, w_output, decay, state):
    all_rows, features = tokens.shape
    size_x, size_y = lax.axis_size("gx"), lax.axis_size("gy")
    chips = size_x // 2
    own_rows = all_rows // size_x
    out_rows = all_rows // size_y
    core = lax.axis_index("gx") % 2
    tokens_f = tokens.astype(jnp.float32)
    scaled_in = (tokens_f * norm_gain).astype(jnp.bfloat16)
    squares = jnp.sum(tokens_f * tokens_f, axis=1, keepdims=True)
    flat_weights = w_project.reshape(features, -1)
    x_split = scaled_in.reshape(chips, 2, own_rows, features)
    s_split = squares.reshape(chips, 2, own_rows, 1)

    def project(which):
        x = lax.dynamic_index_in_dim(x_split, which, 1, False).reshape(-1, features)
        s = lax.dynamic_index_in_dim(s_split, which, 1, False).reshape(-1, 1)
        return jnp.dot(x, flat_weights, preferred_element_type=jnp.float32), s

    def pack(sums, squares):
        high = squares.astype(jnp.bfloat16)
        low = (squares - high.astype(jnp.float32)).astype(jnp.bfloat16)
        tail = jnp.concatenate([high, low], axis=1)
        tail = jnp.pad(tail, ((0, 0), (0, LANES - 2)))
        return jnp.concatenate([sums.astype(jnp.bfloat16), tail], axis=1)

    away = pack(*project(1 - core))
    arrived = lax.ppermute(away, "gx", [(i, i ^ 1) for i in range(size_x)]).astype(jnp.float32)
    sums, own_squares = project(core)
    width = sums.shape[1]
    pair = pack(
        sums + arrived[:, :width],
        own_squares + arrived[:, width : width + 1] + arrived[:, width + 1 : width + 2],
    )
    groups = [[2 * z + c for z in range(chips)] for c in range(2)]
    parts = lax.all_to_all(
        pair.reshape(chips, own_rows, -1), "gx", 0, 0, axis_index_groups=groups
    )
    new_state, gated = pl.pallas_call(
        state_kernel,
        out_shape=(
            jax.ShapeDtypeStruct(state.shape, jnp.float32),
            jax.ShapeDtypeStruct((own_rows, state.shape[1] * HS), jnp.bfloat16),
        ),
        in_specs=[
            pl.BlockSpec(memory_space=pltpu.SMEM),
            pl.BlockSpec(memory_space=pltpu.VMEM),
            pl.BlockSpec(memory_space=pltpu.VMEM),
        ],
        out_specs=(
            pl.BlockSpec(memory_space=pltpu.VMEM),
            pl.BlockSpec(memory_space=pltpu.VMEM),
        ),
        scratch_shapes=[pltpu.VMEM((2, state.shape[1] * HS, own_rows), jnp.float32)],
        compiler_params=pltpu.CompilerParams(vmem_limit_bytes=24 * 2**20),
        name="retention",
    )(decay, parts, state)
    copies = jnp.broadcast_to(gated[None], (size_x,) + gated.shape)
    all_gated = lax.all_to_all(copies, "gx", 0, 0).reshape(all_rows, -1)
    head_terms = jnp.dot(all_gated, w_output, preferred_element_type=jnp.float32)
    terms = lax.all_to_all(
        head_terms.astype(jnp.bfloat16).reshape(size_y, out_rows, -1), "gy", 0, 0
    )
    own_tokens = lax.dynamic_slice_in_dim(tokens_f, lax.axis_index("gy") * out_rows, out_rows, 0)
    own_mixed = (own_tokens + jnp.sum(terms.astype(jnp.float32), axis=0)).astype(jnp.bfloat16)
    copies = jnp.broadcast_to(own_mixed[None], (size_y,) + own_mixed.shape)
    mixed = lax.all_to_all(copies, "gy", 0, 0).reshape(all_rows, -1)
    return (mixed, new_state)


def solution(mesh):
    placed = (
        P(None, "gx"),
        P("gx"),
        P("gx", None, "gy"),
        P("gy", "gx"),
        P("gy"),
        P("gx", "gy", None, None),
    )
    return jax.shard_map(
        local,
        mesh=mesh,
        in_specs=placed,
        out_specs=(P(None, "gx"), P("gx", "gy", None, None)),
        check_vma=False,
    )
```

time: 249 us -> 74.7 us (0.30)
  waiting for transfers between devices: 177 us -> 8.57 us
  between operations: 14.2 us -> 0.84 us
  starting transfers between devices: 0.08 us -> 10.1 us
  other arithmetic: 5.53 us -> 0.43 us
  Pallas kernels: 0 us -> 4.32 us
  local copies, waits for them, and re-layouts: 4.41 us -> 7.08 us
    psum x2 -> x0, waiting for transfers between devices: 177 us -> none  [the longest x1 90.7 us: local(): lax.psum(head_terms.astype(jnp.bfloat16), 'gy').astype(jnp.float32)]
    all_to_all x0 -> x3, blocking collectives: none -> 40.6 us  [the longest x1 18.1 us: local(): lax.all_to_all(pair.reshape(chips, own_rows, -1), 'gx', 0, 0, axis_index_...]
    psum x1 -> x0, blocking collectives: 27.4 us -> none  [local(): totals = lax.psum(squares, 'gx')]
    all_gather x1 -> x0, blocking collectives: 15.6 us -> none  [local(): lax.all_gather(gated, 'gx', axis=0, tiled=True)]
    all_to_all x0 -> x1, waiting for transfers between devices: none -> 7.33 us  [local(): lax.all_to_all(head_terms.astype(jnp.bfloat16).reshape(size_y, out_rows,...]
    all_to_all x0 -> x1, starting transfers between devices: none -> 6.75 us  [local(): lax.all_to_all(head_terms.astype(jnp.bfloat16).reshape(size_y, out_rows,...]
    pallas_call x0 -> x1, Pallas kernels: none -> 4.32 us  [local(): pl.pallas_call(state_kernel, out_shape=(jax.ShapeDtypeStruct(state.shape,...]
    ppermute x0 -> x1, starting transfers between devices: none -> 3.33 us  [local(): lax.ppermute(away, 'gx', [(i, i ^ 1) for i in range(size_x)])]
where the time goes in v1:
time: 74.7 us; the launch traced here: 74.3 us
  blocking collectives  40.6 us (54%)
  starting transfers between devices  10.1 us (14%)
  waiting for transfers between devices  8.57 us (11%)
  local copies, waits for them, and re-layouts  7.08 us (9%)
  Pallas kernels  4.32 us (6%)
  matrix products  2.34 us (3%)
  between operations  0.84 us (1%)
    all_to_all x1, blocking collectives, local(): lax.all_to_all(pair.reshape(chips, own_rows, -1), 'gx', 0, 0, axis_index_...  18.1 us
    all_to_all x1, blocking collectives, local(): all_gated = lax.all_to_all(copies, 'gx', 0, 0).reshape(all_rows, -1)  13 us
    all_to_all x1, blocking collectives, local(): mixed = lax.all_to_all(copies, 'gy', 0, 0).reshape(all_rows, -1)  9.57 us
    all_to_all x1, waiting for transfers between devices, local(): lax.all_to_all(head_terms.astype(jnp.bfloat16).reshape(size_y, out_rows,...  7.33 us
    all_to_all x1, starting transfers between devices, local(): lax.all_to_all(head_terms.astype(jnp.bfloat16).reshape(size_y, out_rows,...  6.75 us
    unnamed x12, local copies, waits for them, and re-layouts  5.13 us
    pallas_call x1, Pallas kernels, local(): pl.pallas_call(state_kernel, out_shape=(jax.ShapeDtypeStruct(state.shape,...  4.32 us
    ppermute x1, starting transfers between devices, local(): lax.ppermute(away, 'gx', [(i, i ^ 1) for i in range(size_x)])  3.33 us
  transfers between devices with their start and end apart: 2, of which 2 were waited for; matrix products, arithmetic and copies ran while one was open for 0% of the time, Pallas kernels for 0%

profile of v1, /device:TPU:1, one launch (start us, length us, event | category | flops | bytes accessed | tf_op | source)
XLA Modules:
  0.0 74.3 jit_solution(1552555904083057859)
XLA Ops:
  0.6 0.0 copy-start
  0.7 0.0 copy-start.3
  0.7 0.0 copy-start.4
  0.7 2.3 %copy.25 = bf16[64,8,4,512]{3,1,2,0:T(8,128)(2,1)S(1)} copy(bf16[64,8,4,512]{3,2,1,0:T(4,128)(2,1)} %bitcast.23) | data formatting | bytes 4194304
  3.0 0.0 copy-done.3
  3.0 0.0 copy-done.4
  3.0 0.1 multiply_convert_fusion
  3.1 0.1 reshape_broadcast_in_dim.3
  3.3 0.1 reshape.81
  3.4 0.1 copy.20
  3.5 0.5 convolution_convert_fusion
  4.0 3.3 %collective-permute-start = (bf16[64,2176]{1,0:T(8,128)(2,1)S(1)}, bf16[64,2176]{1,0:T(8,128)(2,1)}, u32[]{:S(2)}, u32[]{:S(2)}) collective-permute-start(bf16[64,2176]{1,0:T(8,128)(2,1)S(1)} %fusion.3), channel_id=1, source_target_pairs={{0,16},{16,0},{32,48},{48,32},{64,80},{80,64},{96,112},{112,96},{1... | collective-permute-start | bytes 835592 | tf_op jit(solution)/shard_map/ppermute | solution.py:76
  7.3 0.1 reshape.82
  7.4 1.2 %collective-permute-done = bf16[64,2176]{1,0:T(8,128)(2,1)} collective-permute-done((bf16[64,2176]{1,0:T(8,128)(2,1)S(1)}, bf16[64,2176]{1,0:T(8,128)(2,1)}, u32[]{:S(2)}, u32[]{:S(2)}) %collective-permute-start) | collective-permute-done | bytes 278560 | tf_op jit(solution)/shard_map/ppermute | solution.py:76
  8.6 1.3 %copy.21 = bf16[64,2176]{0,1:T(8,128)(2,1)S(1)} copy(bf16[64,2176]{1,0:T(8,128)(2,1)} %collective-permute-done) | data formatting | bytes 557056 | tf_op jit(solution)/shard_map/ppermute | solution.py:76
  9.9 0.1 convert_element_type.79
  10.0 1.0 %fusion.1 = bf16[64,2048]{0,1:T(8,128)(2,1)S(1)} fusion(f32[64,2176]{0,1:T(8,128)S(1)} %convert_element_type.79, bf16[512,2048]{1,0:T(8,128)(2,1)S(1)} %bitcast.22, bf16[8,2,8,512]{3,2,1,0:T(8,128)(2,1)S(1)} %bitcast.26, s32[]{:T(128)S(6)} %select_n.22), kind=kOutput, calls=%fused_computation.4 | convolution fusion | flops 134479872 | bytes 3473412 | tf_op jit(solution)/shard_map/dot_general | solution.py:66
  11.0 0.0 copy-start.2
  11.0 0.1 pad_maximum_fusion
  11.1 0.3 copy.23
  11.4 18.1 %all_to_all.20.parts_ref = bf16[8,8,2176]{2,1,0:T(8,128)(2,1)S(1)} all-to-all(bf16[8,8,2176]{2,1,0:T(8,128)(2,1)S(1)} %bitcast.24), channel_id=1, replica_groups={{0,32,64,96,128,160,192,224},{16,48,80,112,144,176,208,240},{1,33,65,97..., dimensions={0} | all-to-all | bytes 557056 | tf_op jit(solution)/shard_map/all_to_all | solution.py:84
  29.5 0.0 copy-done.2
  29.5 0.0 copy-start.1
  29.5 2.2 %copy-done.1 = f32[8,2,256,256]{3,2,1,0:T(8,128)S(1)} copy-done((f32[8,2,256,256]{3,2,1,0:T(8,128)S(1)}, f32[8,2,256,256]{3,2,1,0:T(8,128)}, u32[]{:S(2)}) %copy-start.1) | copy-done | bytes 4194328
  31.7 4.3 %retention.1 = (f32[8,2,256,256]{3,2,1,0:T(8,128)}, bf16[8,512]{1,0:T(8,128)(2,1)S(1)}) custom-call(f32[2]{0:T(128)S(1)} %copy-done.2, bf16[8,8,2176]{2,1,0:T(8,128)(2,1)S(1)} %all_to_all.20.parts_ref, f32[8,2,256,256]{3,2,1,0:T(8,128)S(1)} %copy-done.1), custom_call_target="tpu_custom_call" | custom-call | tf_op jit(solution)/shard_map/retention/pallas_call | solution.py:87
  36.0 13.0 %all_to_all.21 = bf16[16,8,512]{2,1,0:T(8,128)(2,1)S(1)} all-to-all(bf16[16,8,512]{2,1,0:T(8,128)(2,1)S(1)} %broadcast_in_dim.4), channel_id=1, replica_groups=mesh['gx'=16,'gy'=16] {'gx'}, dimensions={0} | all-to-all | bytes 262144 | tf_op jit(solution)/shard_map/all_to_all | solution.py:107
  49.0 0.0 copy-done
  49.0 0.9 %fusion = bf16[16,8,512]{2,1,0:T(8,128)(2,1)} fusion(bf16[512,512]{1,0:T(8,128)(2,1)S(1)} %copy-done, bf16[16,8,512]{2,1,0:T(8,128)(2,1)S(1)} %all_to_all.21), kind=kOutput, calls=%fused_computation.2 | convolution fusion | flops 67174400 | bytes 786432 | tf_op jit(solution)/shard_map/dot_general | solution.py:108
  49.9 6.8 %all-to-all-start.2 = ((bf16[16,8,512]{2,1,0:T(8,128)(2,1)}), bf16[16,8,512]{2,1,0:T(8,128)(2,1)S(1)}, u32[]{:S(2)}, u32[]{:S(2)}) async-start(bf16[16,8,512]{2,1,0:T(8,128)(2,1)} %fusion), calls=%async_computation.2 | async-start | bytes 262144 | tf_op jit(solution)/shard_map/all_to_all | solution.py:109
  56.7 7.3 %all-to-all-done.2 = bf16[16,8,512]{2,1,0:T(8,128)(2,1)S(1)} async-done(((bf16[16,8,512]{2,1,0:T(8,128)(2,1)}), bf16[16,8,512]{2,1,0:T(8,128)(2,1)S(1)}, u32[]{:S(2)}, u32[]{:S(2)}) %all-to-all-start.2) | async-done | bytes 131104 | tf_op jit(solution)/shard_map/all_to_all | solution.py:109
  64.1 9.6 %all_to_all.22 = bf16[16,8,512]{2,1,0:T(8,128)(2,1)S(1)} all-to-all(bf16[16,8,512]{2,1,0:T(8,128)(2,1)S(1)} %broadcast_in_dim.5), channel_id=1, replica_groups=mesh['gx'=16,'gy'=16] {'gy'}, dimensions={0} | all-to-all | bytes 262144 | tf_op jit(solution)/shard_map/all_to_all | solution.py:115
  73.6 0.7 copy.27
  (12 shorter events, 0.2 us)
Async XLA Ops:
  0.6 48.3 %copy-start = (bf16[512,512]{1,0:T(8,128)(2,1)S(1)}, bf16[512,512]{1,0:T(8,128)(2,1)}, u32[]{:S(2)}) copy-start(bf16[512,512]{1,0:T(8,128)(2,1)} %param.9) | copy-start | bytes 1572868
  0.7 2.3 %copy-start.3 = (bf16[128,512]{1,0:T(8,128)(2,1)S(1)}, bf16[128,512]{1,0:T(8,128)(2,1)}, u32[]{:S(2)}) copy-start(bf16[128,512]{1,0:T(8,128)(2,1)} %param.6) | copy-start | bytes 393220
  0.7 2.3 %copy-start.4 = (f32[512]{0:T(512)S(1)}, f32[512]{0:T(512)}, u32[]{:S(2)}) copy-start(f32[512]{0:T(512)} %param.7) | copy-start | bytes 6148
  4.0 4.6 %collective-permute-start = (bf16[64,2176]{1,0:T(8,128)(2,1)S(1)}, bf16[64,2176]{1,0:T(8,128)(2,1)}, u32[]{:S(2)}, u32[]{:S(2)}) collective-permute-start(bf16[64,2176]{1,0:T(8,128)(2,1)S(1)} %fusion.3), channel_id=1, source_target_pairs={{0,16},{16,0},{32,48},{48,32},{64,80},{80,64},{96,112},{112,96},{1... | collective-permute-start | bytes 835592 | tf_op jit(solution)/shard_map/ppermute | solution.py:76
  11.0 18.5 %copy-start.2 = (f32[2]{0:T(128)S(1)}, f32[2]{0:T(128)}, u32[]{:S(2)}) copy-start(f32[2]{0:T(128)} %decay_ref.1) | copy-start | bytes 28
  29.5 2.2 %copy-start.1 = (f32[8,2,256,256]{3,2,1,0:T(8,128)S(1)}, f32[8,2,256,256]{3,2,1,0:T(8,128)}, u32[]{:S(2)}) copy-start(f32[8,2,256,256]{3,2,1,0:T(8,128)} %state_ref.1) | copy-start | bytes 12582916
  49.9 14.1 %all-to-all-start.2 = ((bf16[16,8,512]{2,1,0:T(8,128)(2,1)}), bf16[16,8,512]{2,1,0:T(8,128)(2,1)S(1)}, u32[]{:S(2)}, u32[]{:S(2)}) async-start(bf16[16,8,512]{2,1,0:T(8,128)(2,1)} %fusion), calls=%async_computation.2 | async-start | bytes 262144 | tf_op jit(solution)/shard_map/all_to_all | solution.py:109

commit v2 on v1

v2 whole, which is shorter than its diff:
```python
import jax
import jax.numpy as jnp
from jax import lax
from jax.experimental import pallas as pl
from jax.experimental.pallas import tpu as pltpu
from jax.sharding import PartitionSpec as P

HS = 256
D = 8192
LANES = 128


def split_squares(squares):
    high = squares.astype(jnp.bfloat16).astype(jnp.float32)
    low = squares - high
    lane = lax.broadcasted_iota(jnp.int32, (squares.shape[0], LANES), 1)
    return jnp.where(lane == 0, high, jnp.where(lane == 1, low, 0.0))


def project_kernel(
    tokens_ref, gain_ref, weights_ref, away_ref, own_ref, kept_ref, scaled_ref, squares_ref
):
    chips, _, rows, features = scaled_ref.shape
    core = lax.rem(lax.axis_index("gx"), 2)
    tokens = tokens_ref[...].astype(jnp.float32)
    squares = jnp.sum(tokens * tokens, axis=1, keepdims=True)
    scaled_ref[...] = (tokens * gain_ref[...]).reshape(scaled_ref.shape)
    squares_ref[...] = jnp.broadcast_to(squares, (tokens.shape[0], LANES)).reshape(squares_ref.shape)
    block = lax.axis_index("gy")
    kept = jnp.zeros(kept_ref.shape, jnp.float32)
    for y in range(tokens.shape[0] // kept.shape[0]):
        kept = jnp.where(block == y, tokens[y * kept.shape[0] : (y + 1) * kept.shape[0]], kept)
    kept_ref[...] = kept
    width = weights_ref.shape[1]
    half = chips * rows
    x = jnp.concatenate(
        [scaled_ref[:, which].reshape(half, features) for which in (1 - core, core)], axis=0
    ).astype(jnp.bfloat16)
    sums = jnp.dot(x, weights_ref[...], preferred_element_type=jnp.float32)
    for n, (which, out_ref) in enumerate(((1 - core, away_ref), (core, own_ref))):
        out_ref[:, :width] = sums[n * half : (n + 1) * half].astype(out_ref.dtype)
        total = squares_ref[:, which].reshape(half, LANES)[:, :1]
        out_ref[:, width:] = split_squares(total).astype(out_ref.dtype)


def pair_kernel(own_ref, arrived_ref, state_ref, pair_ref):
    del state_ref
    width = own_ref.shape[1] - LANES
    pair_ref[:, :width] = (
        own_ref[:, :width] + arrived_ref[:, :width].astype(jnp.float32)
    ).astype(jnp.bfloat16)
    tail = own_ref[:, width:] + arrived_ref[:, width:].astype(jnp.float32)
    total = tail[:, 0:1] + tail[:, 1:2]
    pair_ref[:, width:] = split_squares(total).astype(jnp.bfloat16)


def readout_kernel(
    decay_ref, parts_ref, state_ref, copies_ref, key_cols_ref, values_ref, query_cols_ref
):
    pieces, rows, _ = parts_ref.shape
    heads = state_ref.shape[1]
    width = heads * HS
    summed = parts_ref[0].astype(jnp.float32)
    for z in range(1, pieces):
        summed += parts_ref[z].astype(jnp.float32)
    squares = summed[:, 4 * width : 4 * width + 1] + summed[:, 4 * width + 1 : 4 * width + 2]
    scale = lax.rsqrt(squares / D + 1e-06)
    projected = summed[:, : 4 * width] * scale
    queries = projected[:, :width]
    keys = projected[:, width : 2 * width] * HS ** (-0.5)
    values = projected[:, 2 * width : 3 * width]
    gates = projected[:, 3 * width : 4 * width]
    query_cols_ref[...] = queries.T
    key_cols_ref[...] = keys.T
    values_ref[...] = values
    from_state = [[] for _ in range(heads)]
    for s in range(rows):
        for h in range(heads):
            query_col = query_cols_ref[h * HS : (h + 1) * HS, s : s + 1]
            from_state[h].append(jnp.sum(query_col * state_ref[s, h], axis=0, keepdims=True))
    normed = []
    for h in range(heads):
        here = slice(h * HS, (h + 1) * HS)
        overlap = jnp.sum(queries[:, here] * keys[:, here], axis=1, keepdims=True)
        readout = (
            decay_ref[h] * jnp.concatenate(from_state[h], axis=0) + overlap * values[:, here]
        )
        centre = jnp.mean(readout, axis=1, keepdims=True)
        spread = jnp.mean((readout - centre) ** 2, axis=1, keepdims=True)
        normed.append((readout - centre) * lax.rsqrt(spread + 1e-05))
    gated = gates / (1.0 + jnp.exp(-gates)) * jnp.concatenate(normed, axis=1)
    copies_ref[...] = jnp.broadcast_to(gated.astype(jnp.bfloat16)[None], copies_ref.shape)


def update_kernel(
    decay_ref, key_cols_ref, values_ref, state_ref, new_ref, held_ref, fresh_ref, in_sems, out_sems
):
    rows, heads = state_ref.shape[:2]
    loads = [
        pltpu.make_async_copy(state_ref.at[s], held_ref.at[s], in_sems.at[s]) for s in range(rows)
    ]
    stores = [
        pltpu.make_async_copy(fresh_ref.at[s], new_ref.at[s], out_sems.at[s]) for s in range(rows)
    ]
    for load in loads:
        load.start()
    for s in range(rows):
        loads[s].wait()
        for h in range(heads):
            key_col = key_cols_ref[h * HS : (h + 1) * HS, s : s + 1]
            value_row = values_ref[s : s + 1, h * HS : (h + 1) * HS]
            fresh_ref[s, h] = decay_ref[h] * held_ref[s, h] + key_col * value_row
        stores[s].start()
    for store in stores:
        store.wait()


def finish_kernel(kept_ref, terms_ref, copies_ref):
    total = terms_ref[0].astype(jnp.float32)
    for y in range(1, terms_ref.shape[0]):
        total += terms_ref[y].astype(jnp.float32)
    mixed = (kept_ref[...] + total).astype(jnp.bfloat16)
    copies_ref[...] = jnp.broadcast_to(mixed[None], copies_ref.shape)


def local(tokens, norm_gain, w_project, w_output, decay, state):
    all_rows, features = tokens.shape
    size_x, size_y = lax.axis_size("gx"), lax.axis_size("gy")
    chips = size_x // 2
    own_rows = all_rows // size_x
    out_rows = all_rows // size_y
    heads = state.shape[1]
    flat_weights = w_project.reshape(features, -1)
    padded = flat_weights.shape[1] + LANES
    half = all_rows // 2
    vmem = pl.BlockSpec(memory_space=pltpu.VMEM)
    smem = pl.BlockSpec(memory_space=pltpu.SMEM)
    hbm = pl.BlockSpec(memory_space=pltpu.HBM)
    away, own, kept = pl.pallas_call(
        project_kernel,
        out_shape=(
            jax.ShapeDtypeStruct((half, padded), jnp.bfloat16),
            jax.ShapeDtypeStruct((half, padded), jnp.float32),
            pltpu.VMEM((out_rows, features), jnp.float32),
        ),
        in_specs=[vmem, vmem, vmem],
        out_specs=(vmem, vmem, vmem),
        scratch_shapes=[
            pltpu.VMEM((chips, 2, own_rows, features), jnp.float32),
            pltpu.VMEM((chips, 2, own_rows, LANES), jnp.float32),
        ],
        compiler_params=pltpu.CompilerParams(vmem_limit_bytes=16 * 2**20),
        name="project",
    )(tokens, norm_gain.reshape(1, -1), flat_weights)
    state_hbm = pltpu.with_memory_space_constraint(state, pltpu.HBM)
    arrived = lax.ppermute(away, "gx", [(i, i ^ 1) for i in range(size_x)])
    pair = pl.pallas_call(
        pair_kernel,
        out_shape=jax.ShapeDtypeStruct((half, padded), jnp.bfloat16),
        in_specs=[vmem, vmem, pl.BlockSpec(memory_space=pl.ANY)],
        out_specs=vmem,
        compiler_params=pltpu.CompilerParams(vmem_limit_bytes=16 * 2**20),
        name="pair",
    )(own, arrived, state)
    groups = [[2 * z + c for z in range(chips)] for c in range(2)]
    parts = lax.all_to_all(
        pair.reshape(chips, own_rows, -1), "gx", 0, 0, axis_index_groups=groups
    )
    copies, key_cols, values = pl.pallas_call(
        readout_kernel,
        out_shape=(
            jax.ShapeDtypeStruct((size_x, own_rows, heads * HS), jnp.bfloat16),
            jax.ShapeDtypeStruct((heads * HS, own_rows), jnp.float32),
            jax.ShapeDtypeStruct((own_rows, heads * HS), jnp.float32),
        ),
        in_specs=[smem, vmem, vmem],
        out_specs=(vmem, vmem, vmem),
        scratch_shapes=[pltpu.VMEM((heads * HS, own_rows), jnp.float32)],
        compiler_params=pltpu.CompilerParams(vmem_limit_bytes=24 * 2**20),
        name="readout",
    )(decay, parts, state)
    new_state = pl.pallas_call(
        update_kernel,
        out_shape=jax.ShapeDtypeStruct(state.shape, jnp.float32),
        in_specs=[smem, vmem, vmem, hbm],
        out_specs=hbm,
        scratch_shapes=[
            pltpu.VMEM(state.shape, jnp.float32),
            pltpu.VMEM(state.shape, jnp.float32),
            pltpu.SemaphoreType.DMA((own_rows,)),
            pltpu.SemaphoreType.DMA((own_rows,)),
        ],
        compiler_params=pltpu.CompilerParams(vmem_limit_bytes=24 * 2**20),
        cost_estimate=pl.CostEstimate(flops=2**22, bytes_accessed=2**23, transcendentals=0),
        name="update",
    )(decay, key_cols, values, state_hbm)
    all_gated = lax.all_to_all(copies, "gx", 0, 0).reshape(all_rows, -1)
    head_terms = jnp.dot(all_gated, w_output, preferred_element_type=jnp.float32)
    terms = lax.all_to_all(
        head_terms.astype(jnp.bfloat16).reshape(size_y, out_rows, -1), "gy", 0, 0
    )
    copies = pl.pallas_call(
        finish_kernel,
        out_shape=jax.ShapeDtypeStruct(terms.shape, jnp.bfloat16),
        in_specs=[vmem, vmem],
        out_specs=vmem,
        compiler_params=pltpu.CompilerParams(vmem_limit_bytes=16 * 2**20),
        name="finish",
    )(kept, terms)
    mixed = lax.all_to_all(copies, "gy", 0, 0).reshape(all_rows, -1)
    return (mixed, new_state)


def solution(mesh):
    placed = (
        P(None, "gx"),
        P("gx"),
        P("gx", None, "gy"),
        P("gy", "gx"),
        P("gy"),
        P("gx", "gy", None, None),
    )
    return jax.shard_map(
        local,
        mesh=mesh,
        in_specs=placed,
        out_specs=(P(None, "gx"), P("gx", "gy", None, None)),
        check_vma=False,
    )
```

time: 74.7 us -> 67.3 us (0.901)
  waiting for transfers between devices: 8.57 us -> 4.06 us
  blocking collectives: 40.6 us -> 45 us
  local copies, waits for them, and re-layouts: 7.08 us -> 3.06 us
  starting transfers between devices: 10.1 us -> 6.84 us
  Pallas kernels: 4.32 us -> 7.1 us
  matrix products: 2.34 us -> 0.23 us
    all_to_all x1, waiting for transfers between devices: 7.33 us -> 2.87 us  [local(): mixed = lax.all_to_all(copies, 'gy', 0, 0).reshape(all_rows, -1)]
    all_to_all x1, blocking collectives: 9.57 us -> 13.9 us  [local(): lax.all_to_all(head_terms.astype(jnp.bfloat16).reshape(size_y, out_rows,...]
    all_to_all x1, starting transfers between devices: 6.75 us -> 3.51 us  [local(): mixed = lax.all_to_all(copies, 'gy', 0, 0).reshape(all_rows, -1)]
    pallas_call x1 -> x5, Pallas kernels: 4.32 us -> 7.1 us  [the longest x1 3.92 us: local(): pl.pallas_call(update_kernel, out_shape=jax.ShapeDtypeStruct(state.shape,...]
    unnamed x12, local copies, waits for them, and re-layouts: 5.13 us -> 3.06 us
    dot_general x2 -> x0, matrix products: 1.45 us -> none  [project(): return (jnp.dot(x, flat_weights, preferred_element_type=jnp.float32), s)]
    ppermute x1 -> x0, local copies, waits for them, and re-layouts: 1.27 us -> none  [local(): lax.ppermute(away, 'gx', [(i, i ^ 1) for i in range(size_x)])]
  transfers between devices with their start and end apart: 2 -> 2, of which waited for: 2 -> 2; matrix products, arithmetic and copies ran while one was open for 0% -> 0% of each run, Pallas kernels for 0% -> 6%
where the time goes in v2:
time: 67.3 us; the launch traced here: 67 us
  blocking collectives  45 us (67%)
  Pallas kernels  7.1 us (11%)
  starting transfers between devices  6.84 us (10%)
  waiting for transfers between devices  4.06 us (6%)
  local copies, waits for them, and re-layouts  3.06 us (5%)
  between operations  0.74 us (1%)
    all_to_all x1, blocking collectives, local(): lax.all_to_all(pair.reshape(chips, own_rows, -1), 'gx', 0, 0, axis_index_...  18.1 us
    all_to_all x1, blocking collectives, local(): lax.all_to_all(head_terms.astype(jnp.bfloat16).reshape(size_y, out_rows,...  13.9 us
    all_to_all x1, blocking collectives, local(): all_gated = lax.all_to_all(copies, 'gx', 0, 0).reshape(all_rows, -1)  13 us
    pallas_call x1, Pallas kernels, local(): pl.pallas_call(update_kernel, out_shape=jax.ShapeDtypeStruct(state.shape,...  3.92 us
    all_to_all x1, starting transfers between devices, local(): mixed = lax.all_to_all(copies, 'gy', 0, 0).reshape(all_rows, -1)  3.51 us
    ppermute x1, starting transfers between devices, local(): arrived = lax.ppermute(away, 'gx', [(i, i ^ 1) for i in range(size_x)])  3.33 us
    unnamed x12, local copies, waits for them, and re-layouts  3.06 us
    all_to_all x1, waiting for transfers between devices, local(): mixed = lax.all_to_all(copies, 'gy', 0, 0).reshape(all_rows, -1)  2.87 us
  transfers between devices with their start and end apart: 2, of which 2 were waited for; matrix products, arithmetic and copies ran while one was open for 0% of the time, Pallas kernels for 6%

profile of v2, /device:TPU:1, one launch (start us, length us, event | category | flops | bytes accessed | tf_op | source)
XLA Modules:
  0.0 67.0 jit_solution(14975334504442388213)
XLA Ops:
  0.6 0.0 copy-start
  0.6 0.0 copy-start.3
  0.7 0.0 copy-start.2
  0.7 0.0 copy-start.1
  0.7 2.4 %copy.8 = bf16[64,8,4,512]{3,1,2,0:T(8,128)(2,1)S(1)} copy(bf16[64,8,4,512]{3,2,1,0:T(4,128)(2,1)} %bitcast.14) | data formatting | bytes 4194304
  3.1 0.0 copy-start.4
  3.1 0.0 copy-done.3
  3.1 0.0 copy-done.2
  3.1 0.5 project.1
  3.6 3.3 %collective-permute-start = (bf16[64,2176]{1,0:T(8,128)(2,1)S(1)}, bf16[64,2176]{1,0:T(8,128)(2,1)S(1)}, u32[]{:S(2)}, u32[]{:S(2)}) collective-permute-start(bf16[64,2176]{1,0:T(8,128)(2,1)S(1)} %get-tuple-element.10), channel_id=1, source_target_pairs={{0,16},{16,0},{32,48},{48,32},{64,80},{80,64},{96,112},{112,96},{1... | collective-permute-start | bytes 835592 | tf_op jit(solution)/shard_map/ppermute | solution.py:156
  6.9 1.2 %collective-permute-done.arrived_ref = bf16[64,2176]{1,0:T(8,128)(2,1)S(1)} collective-permute-done((bf16[64,2176]{1,0:T(8,128)(2,1)S(1)}, bf16[64,2176]{1,0:T(8,128)(2,1)S(1)}, u32[]{:S(2)}, u32[]{:S(2)}) %collective-permute-start) | collective-permute-done | bytes 278560 | tf_op jit(solution)/shard_map/ppermute | solution.py:156
  8.1 0.0 copy-done.1
  8.1 0.2 pair.1
  8.3 18.1 %all_to_all.20.parts_ref = bf16[8,8,2176]{2,1,0:T(8,128)(2,1)S(1)} all-to-all(bf16[8,8,2176]{2,1,0:T(8,128)(2,1)S(1)} %bitcast.12), channel_id=1, replica_groups={{0,32,64,96,128,160,192,224},{16,48,80,112,144,176,208,240},{1,33,65,97..., dimensions={0} | all-to-all | bytes 557056 | tf_op jit(solution)/shard_map/all_to_all | solution.py:166
  26.3 0.0 copy-done.4
  26.3 1.8 %readout.1 = (bf16[16,8,512]{2,1,0:T(8,128)(2,1)S(1)}, f32[512,8]{1,0:T(8,128)S(1)}, f32[8,512]{1,0:T(8,128)S(1)}) custom-call(f32[2]{0:T(128)S(1)} %copy-done.4, bf16[8,8,2176]{2,1,0:T(8,128)(2,1)S(1)} %all_to_all.20.parts_ref, f32[8,2,256,256]{3,2,1,0:T(8,128)S(1)} %copy-done.1), custom_call_target="tpu_custom_call" | custom-call | tf_op jit(solution)/shard_map/readout/pallas_call | solution.py:169
  28.2 13.0 %all_to_all.21 = bf16[16,8,512]{2,1,0:T(8,128)(2,1)S(1)} all-to-all(bf16[16,8,512]{2,1,0:T(8,128)(2,1)S(1)} %get-tuple-element.11), channel_id=1, replica_groups=mesh['gx'=16,'gy'=16] {'gx'}, dimensions={0} | all-to-all | bytes 262144 | tf_op jit(solution)/shard_map/all_to_all | solution.py:197
  41.2 0.0 copy-done
  41.2 0.2 fusion
  41.4 13.9 %all_to_all.22.terms_ref = bf16[16,8,512]{2,1,0:T(8,128)(2,1)S(1)} all-to-all(bf16[16,8,512]{2,1,0:T(8,128)(2,1)S(1)} %fusion), channel_id=1, replica_groups=mesh['gx'=16,'gy'=16] {'gy'}, dimensions={0} | all-to-all | bytes 262144 | tf_op jit(solution)/shard_map/all_to_all | solution.py:199
  55.3 0.7 %finish.1 = bf16[16,8,512]{2,1,0:T(8,128)(2,1)} custom-call(f32[8,512]{1,0:T(8,128)S(1)} %get-tuple-element.8.kept_ref, bf16[16,8,512]{2,1,0:T(8,128)(2,1)S(1)} %all_to_all.22.terms_ref), custom_call_target="tpu_custom_call" | custom-call | tf_op jit(solution)/shard_map/finish/pallas_call | solution.py:202
  56.0 3.5 %all-to-all-start.3 = ((bf16[16,8,512]{2,1,0:T(8,128)(2,1)}), bf16[16,8,512]{2,1,0:T(8,128)(2,1)S(1)}, u32[]{:S(2)}, u32[]{:S(2)}) async-start(bf16[16,8,512]{2,1,0:T(8,128)(2,1)} %finish.1), calls=%async_computation.3 | async-start | bytes 262144 | tf_op jit(solution)/shard_map/all_to_all | solution.py:210
  59.5 3.9 %update.1 = f32[8,2,256,256]{3,2,1,0:T(8,128)} custom-call(f32[2]{0:T(128)S(1)} %copy-done.4, f32[512,8]{1,0:T(8,128)S(1)} %get-tuple-element.12.key_cols_ref, f32[8,512]{1,0:T(8,128)S(1)} %get-tuple-element.13.values_ref, f32[8,2,256,256]{3,2,1,0:T(8,128)} %state_ref.5), custom_call_target="tpu_custom_call" | custom-call | flops 4194304 | bytes 8388608 | tf_op jit(solution)/shard_map/update/pallas_call | solution.py:182
  63.4 2.9 %all-to-all-done.3 = bf16[16,8,512]{2,1,0:T(8,128)(2,1)S(1)} async-done(((bf16[16,8,512]{2,1,0:T(8,128)(2,1)}), bf16[16,8,512]{2,1,0:T(8,128)(2,1)S(1)}, u32[]{:S(2)}, u32[]{:S(2)}) %all-to-all-start.3) | async-done | bytes 131104 | tf_op jit(solution)/shard_map/all_to_all | solution.py:210
  66.3 0.7 copy.10
Async XLA Ops:
  0.6 40.5 %copy-start = (bf16[512,512]{1,0:T(8,128)(2,1)S(1)}, bf16[512,512]{1,0:T(8,128)(2,1)}, u32[]{:S(2)}) copy-start(bf16[512,512]{1,0:T(8,128)(2,1)} %param.9) | copy-start | bytes 1572868
  0.6 2.4 %copy-start.3 = (f32[512]{0:T(512)S(1)}, f32[512]{0:T(512)}, u32[]{:S(2)}) copy-start(f32[512]{0:T(512)} %param.7) | copy-start | bytes 6148
  0.7 2.4 %copy-start.2 = (bf16[128,512]{1,0:T(8,128)(2,1)S(1)}, bf16[128,512]{1,0:T(8,128)(2,1)}, u32[]{:S(2)}) copy-start(bf16[128,512]{1,0:T(8,128)(2,1)} %tokens_ref.1) | copy-start | bytes 393220
  0.7 7.4 %copy-start.1 = (f32[8,2,256,256]{3,2,1,0:T(8,128)S(1)}, f32[8,2,256,256]{3,2,1,0:T(8,128)}, u32[]{:S(2)}) copy-start(f32[8,2,256,256]{3,2,1,0:T(8,128)} %state_ref.5) | copy-start | bytes 12582916
  3.1 23.3 %copy-start.4 = (f32[2]{0:T(128)S(1)}, f32[2]{0:T(128)}, u32[]{:S(2)}) copy-start(f32[2]{0:T(128)} %decay_ref.3) | copy-start | bytes 28
  3.6 4.5 %collective-permute-start = (bf16[64,2176]{1,0:T(8,128)(2,1)S(1)}, bf16[64,2176]{1,0:T(8,128)(2,1)S(1)}, u32[]{:S(2)}, u32[]{:S(2)}) collective-permute-start(bf16[64,2176]{1,0:T(8,128)(2,1)S(1)} %get-tuple-element.10), channel_id=1, source_target_pairs={{0,16},{16,0},{32,48},{48,32},{64,80},{80,64},{96,112},{112,96},{1... | collective-permute-start | bytes 835592 | tf_op jit(solution)/shard_map/ppermute | solution.py:156
  56.0 10.3 %all-to-all-start.3 = ((bf16[16,8,512]{2,1,0:T(8,128)(2,1)}), bf16[16,8,512]{2,1,0:T(8,128)(2,1)S(1)}, u32[]{:S(2)}, u32[]{:S(2)}) async-start(bf16[16,8,512]{2,1,0:T(8,128)(2,1)} %finish.1), calls=%async_computation.3 | async-start | bytes 262144 | tf_op jit(solution)/shard_map/all_to_all | solution.py:210

commit v3 on v2

--- a/solution.py
+++ b/solution.py
@@ -17,45 +17,52 @@
     return jnp.where(lane == 0, high, jnp.where(lane == 1, low, 0.0))
 
 
-def project_kernel(
-    tokens_ref, gain_ref, weights_ref, away_ref, own_ref, kept_ref, scaled_ref, squares_ref
+def scale_kernel(
+    tokens_hbm, gain_hbm, scaled_ref, away_squares_ref, own_squares_ref, kept_ref,
+    tokens_ref, gain_ref, rows_ref, squares_ref, sems,
 ):
-    chips, _, rows, features = scaled_ref.shape
+    loads = [
+        pltpu.make_async_copy(tokens_hbm, tokens_ref, sems.at[0]),
+        pltpu.make_async_copy(gain_hbm, gain_ref, sems.at[1]),
+    ]
+    for load in loads:
+        load.start()
+    for load in loads:
+        load.wait()
+    chips, _, rows, features = rows_ref.shape
+    half = chips * rows
     core = lax.rem(lax.axis_index("gx"), 2)
     tokens = tokens_ref[...].astype(jnp.float32)
     squares = jnp.sum(tokens * tokens, axis=1, keepdims=True)
-    scaled_ref[...] = (tokens * gain_ref[...]).reshape(scaled_ref.shape)
+    rows_ref[...] = (tokens * gain_ref[...]).reshape(rows_ref.shape)
     squares_ref[...] = jnp.broadcast_to(squares, (tokens.shape[0], LANES)).reshape(squares_ref.shape)
+    for n, (which, out_ref) in enumerate(
+        ((1 - core, away_squares_ref), (core, own_squares_ref))
+    ):
+        x = rows_ref[:, which].reshape(half, features).astype(jnp.bfloat16)
+        for p in range(scaled_ref.shape[0]):
+            scaled_ref[p, n * half : (n + 1) * half] = x
+        out_ref[...] = squares_ref[:, which].reshape(half, LANES)
     block = lax.axis_index("gy")
     kept = jnp.zeros(kept_ref.shape, jnp.float32)
     for y in range(tokens.shape[0] // kept.shape[0]):
         kept = jnp.where(block == y, tokens[y * kept.shape[0] : (y + 1) * kept.shape[0]], kept)
     kept_ref[...] = kept
-    width = weights_ref.shape[1]
-    half = chips * rows
-    x = jnp.concatenate(
-        [scaled_ref[:, which].reshape(half, features) for which in (1 - core, core)], axis=0
-    ).astype(jnp.bfloat16)
-    sums = jnp.dot(x, weights_ref[...], preferred_element_type=jnp.float32)
-    for n, (which, out_ref) in enumerate(((1 - core, away_ref), (core, own_ref))):
-        out_ref[:, :width] = sums[n * half : (n + 1) * half].astype(out_ref.dtype)
-        total = squares_ref[:, which].reshape(half, LANES)[:, :1]
-        out_ref[:, width:] = split_squares(total).astype(out_ref.dtype)
-
-
-def pair_kernel(own_ref, arrived_ref, state_ref, pair_ref):
+
+
+def pair_kernel(products_ref, arrived_ref, own_ref, other_ref, state_ref, pair_ref):
     del state_ref
-    width = own_ref.shape[1] - LANES
-    pair_ref[:, :width] = (
-        own_ref[:, :width] + arrived_ref[:, :width].astype(jnp.float32)
-    ).astype(jnp.bfloat16)
-    tail = own_ref[:, width:] + arrived_ref[:, width:].astype(jnp.float32)
-    total = tail[:, 0:1] + tail[:, 1:2]
-    pair_ref[:, width:] = split_squares(total).astype(jnp.bfloat16)
+    kinds, half, width = arrived_ref.shape
+    for p in range(kinds):
+        pair_ref[:, p * width : (p + 1) * width] = (
+            products_ref[p, half:].astype(jnp.float32) + arrived_ref[p].astype(jnp.float32)
+        ).astype(jnp.bfloat16)
+    total = (own_ref[...] + other_ref[...])[:, :1]
+    pair_ref[:, kinds * width :] = split_squares(total).astype(jnp.bfloat16)
 
 
 def readout_kernel(
-    decay_ref, parts_ref, state_ref, copies_ref, key_cols_ref, values_ref, query_cols_ref
+    decay_ref, parts_ref, state_ref, copies_ref, keys_ref, values_ref, query_cols_ref
 ):
     pieces, rows, _ = parts_ref.shape
     heads = state_ref.shape[1]
@@ -71,7 +78,7 @@
     values = projected[:, 2 * width : 3 * width]
     gates = projected[:, 3 * width : 4 * width]
     query_cols_ref[...] = queries.T
-    key_cols_ref[...] = keys.T
+    keys_ref[...] = keys
     values_ref[...] = values
     from_state = [[] for _ in range(heads)]
     for s in range(rows):
@@ -93,7 +100,8 @@
 
 
 def update_kernel(
-    decay_ref, key_cols_ref, values_ref, state_ref, new_ref, held_ref, fresh_ref, in_sems, out_sems
+    decay_ref, keys_ref, values_ref, state_ref, new_ref,
+    key_cols_ref, held_ref, fresh_ref, in_sems, out_sems,
 ):
     rows, heads = state_ref.shape[:2]
     loads = [
@@ -104,6 +112,7 @@
     ]
     for load in loads:
         load.start()
+    key_cols_ref[...] = keys_ref[...].T
     for s in range(rows):
         loads[s].wait()
         for h in range(heads):
@@ -130,47 +139,60 @@
     own_rows = all_rows // size_x
     out_rows = all_rows // size_y
     heads = state.shape[1]
-    flat_weights = w_project.reshape(features, -1)
-    padded = flat_weights.shape[1] + LANES
+    kinds, width = w_project.shape[1:]
+    padded = kinds * width + LANES
     half = all_rows // 2
     vmem = pl.BlockSpec(memory_space=pltpu.VMEM)
     smem = pl.BlockSpec(memory_space=pltpu.SMEM)
     hbm = pl.BlockSpec(memory_space=pltpu.HBM)
-    away, own, kept = pl.pallas_call(
-        project_kernel,
+    scaled, away_squares, own_squares, kept = pl.pallas_call(
+        scale_kernel,
         out_shape=(
-            jax.ShapeDtypeStruct((half, padded), jnp.bfloat16),
-            jax.ShapeDtypeStruct((half, padded), jnp.float32),
+            pltpu.VMEM((kinds, all_rows, features), jnp.bfloat16),
+            pltpu.VMEM((half, LANES), jnp.float32),
+            pltpu.VMEM((half, LANES), jnp.float32),
             pltpu.VMEM((out_rows, features), jnp.float32),
         ),
-        in_specs=[vmem, vmem, vmem],
-        out_specs=(vmem, vmem, vmem),
+        in_specs=[hbm, hbm],
+        out_specs=(vmem, vmem, vmem, vmem),
         scratch_shapes=[
+            pltpu.VMEM(tokens.shape, tokens.dtype),
+            pltpu.VMEM((1, features), jnp.float32),
             pltpu.VMEM((chips, 2, own_rows, features), jnp.float32),
             pltpu.VMEM((chips, 2, own_rows, LANES), jnp.float32),
+            pltpu.SemaphoreType.DMA((2,)),
         ],
         compiler_params=pltpu.CompilerParams(vmem_limit_bytes=16 * 2**20),
-        name="project",
-    )(tokens, norm_gain.reshape(1, -1), flat_weights)
+        cost_estimate=pl.CostEstimate(flops=2**33, bytes_accessed=2**18, transcendentals=0),
+        name="scale",
+    )(
+        pltpu.with_memory_space_constraint(tokens, pltpu.HBM),
+        pltpu.with_memory_space_constraint(norm_gain.reshape(1, -1), pltpu.HBM),
+    )
+    products = jnp.einsum(
+        "psi,ipo->pso", scaled, w_project, preferred_element_type=jnp.float32
+    ).astype(jnp.bfloat16)
     state_hbm = pltpu.with_memory_space_constraint(state, pltpu.HBM)
-    arrived = lax.ppermute(away, "gx", [(i, i ^ 1) for i in range(size_x)])
+    swap = [(i, i ^ 1) for i in range(size_x)]
+    other_squares = lax.ppermute(away_squares, "gx", swap)
+    arrived = lax.ppermute(products[:, :half], "gx", swap)
     pair = pl.pallas_call(
         pair_kernel,
         out_shape=jax.ShapeDtypeStruct((half, padded), jnp.bfloat16),
-        in_specs=[vmem, vmem, pl.BlockSpec(memory_space=pl.ANY)],
+        in_specs=[vmem, vmem, vmem, vmem, pl.BlockSpec(memory_space=pl.ANY)],
         out_specs=vmem,
         compiler_params=pltpu.CompilerParams(vmem_limit_bytes=16 * 2**20),
         name="pair",
-    )(own, arrived, state)
+    )(products, arrived, own_squares, other_squares, state)
     groups = [[2 * z + c for z in range(chips)] for c in range(2)]
     parts = lax.all_to_all(
         pair.reshape(chips, own_rows, -1), "gx", 0, 0, axis_index_groups=groups
     )
-    copies, key_cols, values = pl.pallas_call(
+    copies, keys, values = pl.pallas_call(
         readout_kernel,
         out_shape=(
             jax.ShapeDtypeStruct((size_x, own_rows, heads * HS), jnp.bfloat16),
-            jax.ShapeDtypeStruct((heads * HS, own_rows), jnp.float32),
+            jax.ShapeDtypeStruct((own_rows, heads * HS), jnp.float32),
             jax.ShapeDtypeStruct((own_rows, heads * HS), jnp.float32),
         ),
         in_specs=[smem, vmem, vmem],
@@ -185,6 +207,7 @@
         in_specs=[smem, vmem, vmem, hbm],
         out_specs=hbm,
         scratch_shapes=[
+            pltpu.VMEM((heads * HS, own_rows), jnp.float32),
             pltpu.VMEM(state.shape, jnp.float32),
             pltpu.VMEM(state.shape, jnp.float32),
             pltpu.SemaphoreType.DMA((own_rows,)),
@@ -193,7 +216,7 @@
         compiler_params=pltpu.CompilerParams(vmem_limit_bytes=24 * 2**20),
         cost_estimate=pl.CostEstimate(flops=2**22, bytes_accessed=2**23, transcendentals=0),
         name="update",
-    )(decay, key_cols, values, state_hbm)
+    )(decay, keys, values, state_hbm)
     all_gated = lax.all_to_all(copies, "gx", 0, 0).reshape(all_rows, -1)
     head_terms = jnp.dot(all_gated, w_output, preferred_element_type=jnp.float32)
     terms = lax.all_to_all(

time: 67.3 us -> 66.7 us (level)
  local copies, waits for them, and re-layouts: 3.06 us -> 1.09 us
  matrix products: 0.23 us -> 0.98 us
    unnamed x12 -> x9, local copies, waits for them, and re-layouts: 3.06 us -> 1.07 us
    pallas_call x1, Pallas kernels: 0.48 us -> 1.25 us  [local(): pl.pallas_call(scale_kernel, out_shape=(pltpu.VMEM((kinds, all_rows, feat...]
    dot_general x0 -> x1, matrix products: none -> 0.75 us  [local(): jnp.einsum('psi,ipo->pso', scaled, w_project, preferred_element_type=jnp....]
    ppermute x1 -> x2, starting transfers between devices: 3.33 us -> 3.43 us  [the longest x1 3.33 us: local(): arrived = lax.ppermute(products[:, :half], 'gx', swap)]
  transfers between devices with their start and end apart: 2 -> 3, of which waited for: 2 -> 2; matrix products, arithmetic and copies ran while one was open for 0% -> 0% of each run, Pallas kernels for 6% -> 6%
where the time goes in v3:
time: 66.7 us; the launch traced here: 66.4 us
  blocking collectives  45 us (67%)
  Pallas kernels  7.74 us (12%)
  starting transfers between devices  6.94 us (10%)
  waiting for transfers between devices  3.98 us (6%)
  local copies, waits for them, and re-layouts  1.09 us (2%)
  matrix products  0.98 us (1%)
  between operations  0.71 us (1%)
    all_to_all x1, blocking collectives, local(): lax.all_to_all(pair.reshape(chips, own_rows, -1), 'gx', 0, 0, axis_index_...  18.1 us
    all_to_all x1, blocking collectives, local(): lax.all_to_all(head_terms.astype(jnp.bfloat16).reshape(size_y, out_rows,...  13.9 us
    all_to_all x1, blocking collectives, local(): all_gated = lax.all_to_all(copies, 'gx', 0, 0).reshape(all_rows, -1)  13 us
    pallas_call x1, Pallas kernels, local(): pl.pallas_call(update_kernel, out_shape=jax.ShapeDtypeStruct(state.shape,...  3.92 us
    all_to_all x1, starting transfers between devices, local(): mixed = lax.all_to_all(copies, 'gy', 0, 0).reshape(all_rows, -1)  3.51 us
    ppermute x1, starting transfers between devices, local(): arrived = lax.ppermute(products[:, :half], 'gx', swap)  3.33 us
    all_to_all x1, waiting for transfers between devices, local(): mixed = lax.all_to_all(copies, 'gy', 0, 0).reshape(all_rows, -1)  2.87 us
    pallas_call x1, Pallas kernels, local(): pl.pallas_call(readout_kernel, out_shape=(jax.ShapeDtypeStruct((size_x, o...  1.8 us
  transfers between devices with their start and end apart: 3, of which 2 were waited for; matrix products, arithmetic and copies ran while one was open for 0% of the time, Pallas kernels for 6%

profile of v3, /device:TPU:1, one launch (start us, length us, event | category | flops | bytes accessed | tf_op | source)
XLA Modules:
  0.0 66.4 jit_solution(5112441089091440611)
XLA Ops:
  0.6 0.0 copy-start
  0.6 0.0 copy-start.1
  0.7 1.2 %scale.1 = (bf16[4,128,512]{2,1,0:T(8,128)(2,1)S(1)}, f32[64,128]{1,0:T(8,128)S(1)}, f32[64,128]{1,0:T(8,128)S(1)}, f32[8,512]{1,0:T(8,128)S(1)}) custom-call(bf16[128,512]{1,0:T(8,128)(2,1)} %tokens_hbm.1, f32[1,512]{1,0:T(1,128)} %bitcast.12), custom_call_target="tpu_custom_call" | custom-call | flops 8589934592 | bytes 262144 | tf_op jit(solution)/shard_map/scale/pallas_call | solution.py:148
  1.9 0.4 copy-done
  2.3 0.8 %fusion.2.products_ref = bf16[4,128,512]{2,1,0:T(8,128)(2,1)S(1)} fusion(bf16[4,128,512]{2,1,0:T(8,128)(2,1)S(1)} %get-tuple-element.10, bf16[512,4,512]{2,1,0:T(4,128)(2,1)S(1)} %copy-done), kind=kOutput, calls=%fused_computation.2 | convolution fusion | flops 268697600 | bytes 3145728 | tf_op jit(solution)/shard_map/psi,ipo->pso/dot_general | solution.py:172
  3.1 3.3 %collective-permute-start = (bf16[4,64,512]{2,1,0:T(8,128)(2,1)S(1)}, bf16[4,64,512]{2,1,0:T(8,128)(2,1)S(1)}, u32[]{:S(2)}, u32[]{:S(2)}) collective-permute-start(bf16[4,64,512]{2,1,0:T(8,128)(2,1)S(1)} %slice.4), channel_id=1, source_target_pairs={{0,16},{16,0},{32,48},{48,32},{64,80},{80,64},{96,112},{112,96},{1... | collective-permute-start | bytes 786440 | tf_op jit(solution)/shard_map/ppermute | solution.py:178
  6.4 0.1 collective-permute-start.1
  6.5 1.1 %collective-permute-done.1.other_ref = f32[64,128]{1,0:T(8,128)S(1)} collective-permute-done((f32[64,128]{1,0:T(8,128)S(1)}, f32[64,128]{1,0:T(8,128)S(1)}, u32[]{:S(2)}, u32[]{:S(2)}) %collective-permute-start.1) | collective-permute-done | bytes 32800 | tf_op jit(solution)/shard_map/ppermute | solution.py:177
  7.6 0.0 collective-permute-done.arrived_ref
  7.6 0.0 copy-done.1
  7.6 0.0 copy-start.2
  7.6 0.1 pair.1
  7.7 18.1 %all_to_all.20.parts_ref = bf16[8,8,2176]{2,1,0:T(8,128)(2,1)S(1)} all-to-all(bf16[8,8,2176]{2,1,0:T(8,128)(2,1)S(1)} %bitcast.10), channel_id=1, replica_groups={{0,32,64,96,128,160,192,224},{16,48,80,112,144,176,208,240},{1,33,65,97..., dimensions={0} | all-to-all | bytes 557056 | tf_op jit(solution)/shard_map/all_to_all | solution.py:188
  25.8 0.0 copy-done.2
  25.8 0.0 copy-start.3
  25.8 1.8 %readout.1 = (bf16[16,8,512]{2,1,0:T(8,128)(2,1)S(1)}, f32[8,512]{1,0:T(8,128)S(1)}, f32[8,512]{1,0:T(8,128)S(1)}) custom-call(f32[2]{0:T(128)S(1)} %copy-done.2, bf16[8,8,2176]{2,1,0:T(8,128)(2,1)S(1)} %all_to_all.20.parts_ref, f32[8,2,256,256]{3,2,1,0:T(8,128)S(1)} %copy-done.1), custom_call_target="tpu_custom_call" | custom-call | tf_op jit(solution)/shard_map/readout/pallas_call | solution.py:191
  27.6 13.0 %all_to_all.21 = bf16[16,8,512]{2,1,0:T(8,128)(2,1)S(1)} all-to-all(bf16[16,8,512]{2,1,0:T(8,128)(2,1)S(1)} %get-tuple-element.13), channel_id=1, replica_groups=mesh['gx'=16,'gy'=16] {'gx'}, dimensions={0} | all-to-all | bytes 262144 | tf_op jit(solution)/shard_map/all_to_all | solution.py:220
  40.6 0.0 copy-done.3
  40.6 0.2 fusion.5
  40.8 13.9 %all_to_all.22.terms_ref = bf16[16,8,512]{2,1,0:T(8,128)(2,1)S(1)} all-to-all(bf16[16,8,512]{2,1,0:T(8,128)(2,1)S(1)} %fusion.5), channel_id=1, replica_groups=mesh['gx'=16,'gy'=16] {'gy'}, dimensions={0} | all-to-all | bytes 262144 | tf_op jit(solution)/shard_map/all_to_all | solution.py:222
  54.7 0.7 %finish.1 = bf16[16,8,512]{2,1,0:T(8,128)(2,1)} custom-call(f32[8,512]{1,0:T(8,128)S(1)} %get-tuple-element.9.kept_ref, bf16[16,8,512]{2,1,0:T(8,128)(2,1)S(1)} %all_to_all.22.terms_ref), custom_call_target="tpu_custom_call" | custom-call | tf_op jit(solution)/shard_map/finish/pallas_call | solution.py:225
  55.4 3.5 %all-to-all-start.3 = ((bf16[16,8,512]{2,1,0:T(8,128)(2,1)}), bf16[16,8,512]{2,1,0:T(8,128)(2,1)S(1)}, u32[]{:S(2)}, u32[]{:S(2)}) async-start(bf16[16,8,512]{2,1,0:T(8,128)(2,1)} %finish.1), calls=%async_computation.3 | async-start | bytes 262144 | tf_op jit(solution)/shard_map/all_to_all | solution.py:233
  58.9 3.9 %update.1 = f32[8,2,256,256]{3,2,1,0:T(8,128)} custom-call(f32[2]{0:T(128)S(1)} %copy-done.2, f32[8,512]{1,0:T(8,128)S(1)} %get-tuple-element.14.keys_ref, f32[8,512]{1,0:T(8,128)S(1)} %get-tuple-element.15.values_ref, f32[8,2,256,256]{3,2,1,0:T(8,128)} %state_ref.5), custom_call_target="tpu_custom_call" | custom-call | flops 4194304 | bytes 8388608 | tf_op jit(solution)/shard_map/update/pallas_call | solution.py:204
  62.9 2.9 %all-to-all-done.3 = bf16[16,8,512]{2,1,0:T(8,128)(2,1)S(1)} async-done(((bf16[16,8,512]{2,1,0:T(8,128)(2,1)}), bf16[16,8,512]{2,1,0:T(8,128)(2,1)S(1)}, u32[]{:S(2)}, u32[]{:S(2)}) %all-to-all-start.3) | async-done | bytes 131104 | tf_op jit(solution)/shard_map/all_to_all | solution.py:233
  65.8 0.7 copy.14
  (1 shorter events, 0.0 us)
Async XLA Ops:
  0.6 1.7 %copy-start = (bf16[512,4,512]{2,1,0:T(4,128)(2,1)S(1)}, bf16[512,4,512]{2,1,0:T(4,128)(2,1)}, u32[]{:S(2)}) copy-start(bf16[512,4,512]{2,1,0:T(4,128)(2,1)} %param.8) | copy-start | bytes 6291460
  0.6 7.0 %copy-start.1 = (f32[8,2,256,256]{3,2,1,0:T(8,128)S(1)}, f32[8,2,256,256]{3,2,1,0:T(8,128)}, u32[]{:S(2)}) copy-start(f32[8,2,256,256]{3,2,1,0:T(8,128)} %state_ref.5) | copy-start | bytes 12582916
  3.1 4.5 %collective-permute-start = (bf16[4,64,512]{2,1,0:T(8,128)(2,1)S(1)}, bf16[4,64,512]{2,1,0:T(8,128)(2,1)S(1)}, u32[]{:S(2)}, u32[]{:S(2)}) collective-permute-start(bf16[4,64,512]{2,1,0:T(8,128)(2,1)S(1)} %slice.4), channel_id=1, source_target_pairs={{0,16},{16,0},{32,48},{48,32},{64,80},{80,64},{96,112},{112,96},{1... | collective-permute-start | bytes 786440 | tf_op jit(solution)/shard_map/ppermute | solution.py:178
  6.4 1.2 %collective-permute-start.1 = (f32[64,128]{1,0:T(8,128)S(1)}, f32[64,128]{1,0:T(8,128)S(1)}, u32[]{:S(2)}, u32[]{:S(2)}) collective-permute-start(f32[64,128]{1,0:T(8,128)S(1)} %get-tuple-element.12), channel_id=1, source_target_pairs={{0,16},{16,0},{32,48},{48,32},{64,80},{80,64},{96,112},{112,96},{1... | collective-permute-start | bytes 98312 | tf_op jit(solution)/shard_map/ppermute | solution.py:177
  7.6 18.2 %copy-start.2 = (f32[2]{0:T(128)S(1)}, f32[2]{0:T(128)}, u32[]{:S(2)}) copy-start(f32[2]{0:T(128)} %decay_ref.3) | copy-start | bytes 28
  25.8 14.8 %copy-start.3 = (bf16[512,512]{1,0:T(8,128)(2,1)S(1)}, bf16[512,512]{1,0:T(8,128)(2,1)}, u32[]{:S(2)}) copy-start(bf16[512,512]{1,0:T(8,128)(2,1)} %param.9) | copy-start | bytes 1572868
  55.4 10.3 %all-to-all-start.3 = ((bf16[16,8,512]{2,1,0:T(8,128)(2,1)}), bf16[16,8,512]{2,1,0:T(8,128)(2,1)S(1)}, u32[]{:S(2)}, u32[]{:S(2)}) async-start(bf16[16,8,512]{2,1,0:T(8,128)(2,1)} %finish.1), calls=%async_computation.3 | async-start | bytes 262144 | tf_op jit(solution)/shard_map/all_to_all | solution.py:233

commit v4 on v3

--- a/solution.py
+++ b/solution.py
@@ -18,7 +18,7 @@
 
 
 def scale_kernel(
-    tokens_hbm, gain_hbm, scaled_ref, away_squares_ref, own_squares_ref, kept_ref,
+    tokens_hbm, gain_hbm, scaled_ref, away_squares_ref, own_squares_ref,
     tokens_ref, gain_ref, rows_ref, squares_ref, sems,
 ):
     loads = [
@@ -43,11 +43,6 @@
         for p in range(scaled_ref.shape[0]):
             scaled_ref[p, n * half : (n + 1) * half] = x
         out_ref[...] = squares_ref[:, which].reshape(half, LANES)
-    block = lax.axis_index("gy")
-    kept = jnp.zeros(kept_ref.shape, jnp.float32)
-    for y in range(tokens.shape[0] // kept.shape[0]):
-        kept = jnp.where(block == y, tokens[y * kept.shape[0] : (y + 1) * kept.shape[0]], kept)
-    kept_ref[...] = kept
 
 
 def pair_kernel(products_ref, arrived_ref, own_ref, other_ref, state_ref, pair_ref):
@@ -77,7 +72,7 @@
     keys = projected[:, width : 2 * width] * HS ** (-0.5)
     values = projected[:, 2 * width : 3 * width]
     gates = projected[:, 3 * width : 4 * width]
-    query_cols_ref[...] = queries.T
+    query_cols_ref[...] = summed[:, :width].T
     keys_ref[...] = keys
     values_ref[...] = values
     from_state = [[] for _ in range(heads)]
@@ -90,7 +85,8 @@
         here = slice(h * HS, (h + 1) * HS)
         overlap = jnp.sum(queries[:, here] * keys[:, here], axis=1, keepdims=True)
         readout = (
-            decay_ref[h] * jnp.concatenate(from_state[h], axis=0) + overlap * values[:, here]
+            decay_ref[h] * scale * jnp.concatenate(from_state[h], axis=0)
+            + overlap * values[:, here]
         )
         centre = jnp.mean(readout, axis=1, keepdims=True)
         spread = jnp.mean((readout - centre) ** 2, axis=1, keepdims=True)
@@ -124,12 +120,20 @@
         store.wait()
 
 
-def finish_kernel(kept_ref, terms_ref, copies_ref):
+def middle_kernel(terms_ref, copies_ref):
     total = terms_ref[0].astype(jnp.float32)
-    for y in range(1, terms_ref.shape[0]):
-        total += terms_ref[y].astype(jnp.float32)
-    mixed = (kept_ref[...] + total).astype(jnp.bfloat16)
-    copies_ref[...] = jnp.broadcast_to(mixed[None], copies_ref.shape)
+    for n in range(1, terms_ref.shape[0]):
+        total += terms_ref[n].astype(jnp.float32)
+    copies_ref[...] = jnp.broadcast_to(total.astype(jnp.bfloat16)[None], copies_ref.shape)
+
+
+def finish_kernel(tokens_ref, terms_ref, mixed_ref):
+    blocks, rows, _ = terms_ref.shape
+    blocks //= 2
+    for n in range(blocks):
+        here = slice(n * rows, (n + 1) * rows)
+        total = terms_ref[n].astype(jnp.float32) + terms_ref[blocks + n].astype(jnp.float32)
+        mixed_ref[here] = (tokens_ref[here].astype(jnp.float32) + total).astype(jnp.bfloat16)
 
 
 def local(tokens, norm_gain, w_project, w_output, decay, state):
@@ -137,7 +141,6 @@
     size_x, size_y = lax.axis_size("gx"), lax.axis_size("gy")
     chips = size_x // 2
     own_rows = all_rows // size_x
-    out_rows = all_rows // size_y
     heads = state.shape[1]
     kinds, width = w_project.shape[1:]
     padded = kinds * width + LANES
@@ -145,16 +148,15 @@
     vmem = pl.BlockSpec(memory_space=pltpu.VMEM)
     smem = pl.BlockSpec(memory_space=pltpu.SMEM)
     hbm = pl.BlockSpec(memory_space=pltpu.HBM)
-    scaled, away_squares, own_squares, kept = pl.pallas_call(
+    scaled, away_squares, own_squares = pl.pallas_call(
         scale_kernel,
         out_shape=(
             pltpu.VMEM((kinds, all_rows, features), jnp.bfloat16),
             pltpu.VMEM((half, LANES), jnp.float32),
             pltpu.VMEM((half, LANES), jnp.float32),
-            pltpu.VMEM((out_rows, features), jnp.float32),
         ),
         in_specs=[hbm, hbm],
-        out_specs=(vmem, vmem, vmem, vmem),
+        out_specs=(vmem, vmem, vmem),
         scratch_shapes=[
             pltpu.VMEM(tokens.shape, tokens.dtype),
             pltpu.VMEM((1, features), jnp.float32),
@@ -219,18 +221,29 @@
     )(decay, keys, values, state_hbm)
     all_gated = lax.all_to_all(copies, "gx", 0, 0).reshape(all_rows, -1)
     head_terms = jnp.dot(all_gated, w_output, preferred_element_type=jnp.float32)
+    blocks = size_y // 2
+    halves = [list(range(blocks)), list(range(blocks, size_y))]
+    params = pltpu.CompilerParams(vmem_limit_bytes=16 * 2**20)
     terms = lax.all_to_all(
-        head_terms.astype(jnp.bfloat16).reshape(size_y, out_rows, -1), "gy", 0, 0
+        head_terms.astype(jnp.bfloat16).reshape(blocks, all_rows // blocks, features),
+        "gy", 0, 0, axis_index_groups=halves,
     )
     copies = pl.pallas_call(
+        middle_kernel,
+        out_shape=jax.ShapeDtypeStruct((size_y,) + terms.shape[1:], jnp.bfloat16),
+        in_specs=[vmem],
+        out_specs=vmem,
+        compiler_params=params,
+        name="middle",
+    )(terms)
+    mixed = pl.pallas_call(
         finish_kernel,
-        out_shape=jax.ShapeDtypeStruct(terms.shape, jnp.bfloat16),
+        out_shape=jax.ShapeDtypeStruct((all_rows, features), jnp.bfloat16),
         in_specs=[vmem, vmem],
         out_specs=vmem,
-        compiler_params=pltpu.CompilerParams(vmem_limit_bytes=16 * 2**20),
+        compiler_params=params,
         name="finish",
-    )(kept, terms)
-    mixed = lax.all_to_all(copies, "gy", 0, 0).reshape(all_rows, -1)
+    )(tokens, lax.all_to_all(copies, "gy", 0, 0))
     return (mixed, new_state)
 
 

time: 66.7 us -> 65.4 us (0.981)
  blocking collectives: 45 us -> 41.3 us
  starting transfers between devices: 6.94 us -> 8.3 us
  waiting for transfers between devices: 3.98 us -> 4.71 us
    all_to_all x1, blocking collectives: 13.9 us -> 10.3 us  [local(): lax.all_to_all(head_terms.astype(jnp.bfloat16).reshape(blocks, all_rows /...]
    all_to_all x1, starting transfers between devices: 3.51 us -> 4.87 us  [local(): lax.all_to_all(copies, 'gy', 0, 0)]
    pallas_call x1 -> x2, Pallas kernels: 0.68 us -> 1.45 us  [the longest x1 0.75 us: local(): pl.pallas_call(middle_kernel, out_shape=jax.ShapeDtypeStruct((size_y,) +...]
    all_to_all x1, waiting for transfers between devices: 2.87 us -> 3.6 us  [local(): lax.all_to_all(copies, 'gy', 0, 0)]
where the time goes in v4:
time: 65.4 us; the launch traced here: 64.9 us
  blocking collectives  41.3 us (63%)
  Pallas kernels  8.36 us (13%)
  starting transfers between devices  8.3 us (13%)
  waiting for transfers between devices  4.71 us (7%)
  matrix products  0.98 us (1%)
  between operations  0.72 us (1%)
    all_to_all x1, blocking collectives, local(): lax.all_to_all(pair.reshape(chips, own_rows, -1), 'gx', 0, 0, axis_index_...  18.1 us
    all_to_all x1, blocking collectives, local(): all_gated = lax.all_to_all(copies, 'gx', 0, 0).reshape(all_rows, -1)  13 us
    all_to_all x1, blocking collectives, local(): lax.all_to_all(head_terms.astype(jnp.bfloat16).reshape(blocks, all_rows /...  10.3 us
    all_to_all x1, starting transfers between devices, local(): lax.all_to_all(copies, 'gy', 0, 0)  4.87 us
    pallas_call x1, Pallas kernels, local(): pl.pallas_call(update_kernel, out_shape=jax.ShapeDtypeStruct(state.shape,...  3.92 us
    all_to_all x1, waiting for transfers between devices, local(): lax.all_to_all(copies, 'gy', 0, 0)  3.6 us
    ppermute x1, starting transfers between devices, local(): arrived = lax.ppermute(products[:, :half], 'gx', swap)  3.33 us
    pallas_call x1, Pallas kernels, local(): pl.pallas_call(readout_kernel, out_shape=(jax.ShapeDtypeStruct((size_x, o...  1.67 us
  transfers between devices with their start and end apart: 3, of which 2 were waited for; matrix products, arithmetic and copies ran while one was open for 0% of the time, Pallas kernels for 6%

profile of v4, /device:TPU:1, one launch (start us, length us, event | category | flops | bytes accessed | tf_op | source)
XLA Modules:
  0.0 64.9 jit_solution(5700933015894170609)
XLA Ops:
  0.6 0.0 copy-start
  0.6 0.0 copy-start.1
  0.7 1.2 %scale.1 = (bf16[4,128,512]{2,1,0:T(8,128)(2,1)S(1)}, f32[64,128]{1,0:T(8,128)S(1)}, f32[64,128]{1,0:T(8,128)S(1)}) custom-call(bf16[128,512]{1,0:T(8,128)(2,1)} %tokens_ref.1, f32[1,512]{1,0:T(1,128)} %bitcast.10), custom_call_target="tpu_custom_call" | custom-call | flops 8589934592 | bytes 262144 | tf_op jit(solution)/shard_map/scale/pallas_call | solution.py:151
  1.9 0.4 copy-done
  2.3 0.8 %fusion.2.products_ref = bf16[4,128,512]{2,1,0:T(8,128)(2,1)S(1)} fusion(bf16[4,128,512]{2,1,0:T(8,128)(2,1)S(1)} %get-tuple-element.8, bf16[512,4,512]{2,1,0:T(4,128)(2,1)S(1)} %copy-done), kind=kOutput, calls=%fused_computation.2 | convolution fusion | flops 268697600 | bytes 3145728 | tf_op jit(solution)/shard_map/psi,ipo->pso/dot_general | solution.py:174
  3.1 3.3 %collective-permute-start = (bf16[4,64,512]{2,1,0:T(8,128)(2,1)S(1)}, bf16[4,64,512]{2,1,0:T(8,128)(2,1)S(1)}, u32[]{:S(2)}, u32[]{:S(2)}) collective-permute-start(bf16[4,64,512]{2,1,0:T(8,128)(2,1)S(1)} %slice.4), channel_id=1, source_target_pairs={{0,16},{16,0},{32,48},{48,32},{64,80},{80,64},{96,112},{112,96},{1... | collective-permute-start | bytes 786440 | tf_op jit(solution)/shard_map/ppermute | solution.py:180
  6.4 0.1 collective-permute-start.1
  6.5 1.1 %collective-permute-done.1.other_ref = f32[64,128]{1,0:T(8,128)S(1)} collective-permute-done((f32[64,128]{1,0:T(8,128)S(1)}, f32[64,128]{1,0:T(8,128)S(1)}, u32[]{:S(2)}, u32[]{:S(2)}) %collective-permute-start.1) | collective-permute-done | bytes 32800 | tf_op jit(solution)/shard_map/ppermute | solution.py:179
  7.6 0.0 collective-permute-done.arrived_ref
  7.6 0.0 copy-done.1
  7.6 0.0 copy-start.3
  7.6 0.1 pair.1
  7.7 18.1 %all_to_all.20.parts_ref = bf16[8,8,2176]{2,1,0:T(8,128)(2,1)S(1)} all-to-all(bf16[8,8,2176]{2,1,0:T(8,128)(2,1)S(1)} %bitcast.8), channel_id=1, replica_groups={{0,32,64,96,128,160,192,224},{16,48,80,112,144,176,208,240},{1,33,65,97..., dimensions={0} | all-to-all | bytes 557056 | tf_op jit(solution)/shard_map/all_to_all | solution.py:190
  25.8 0.0 copy-done.3
  25.8 0.0 copy-start.4
  25.8 1.7 %readout.1 = (bf16[16,8,512]{2,1,0:T(8,128)(2,1)S(1)}, f32[8,512]{1,0:T(8,128)S(1)}, f32[8,512]{1,0:T(8,128)S(1)}) custom-call(f32[2]{0:T(128)S(1)} %copy-done.3, bf16[8,8,2176]{2,1,0:T(8,128)(2,1)S(1)} %all_to_all.20.parts_ref, f32[8,2,256,256]{3,2,1,0:T(8,128)S(1)} %copy-done.1), custom_call_target="tpu_custom_call" | custom-call | tf_op jit(solution)/shard_map/readout/pallas_call | solution.py:193
  27.5 13.0 %all_to_all.21 = bf16[16,8,512]{2,1,0:T(8,128)(2,1)S(1)} all-to-all(bf16[16,8,512]{2,1,0:T(8,128)(2,1)S(1)} %get-tuple-element.11), channel_id=1, replica_groups=mesh['gx'=16,'gy'=16] {'gx'}, dimensions={0} | all-to-all | bytes 262144 | tf_op jit(solution)/shard_map/all_to_all | solution.py:222
  40.5 0.0 copy-done.4
  40.5 0.2 convolution_convert_fusion
  40.7 10.3 %all_to_all.22.terms_ref = bf16[8,16,512]{2,1,0:T(8,128)(2,1)S(1)} all-to-all(bf16[8,16,512]{2,1,0:T(8,128)(2,1)S(1)} %bitcast.9), channel_id=1, replica_groups={{0,1,2,3,4,5,6,7},{8,9,10,11,12,13,14,15},{16,17,18,19,20,21,22,23},{24..., dimensions={0} | all-to-all | bytes 262144 | tf_op jit(solution)/shard_map/all_to_all | solution.py:227
  51.0 0.7 %middle.1 = bf16[16,16,512]{2,1,0:T(8,128)(2,1)} custom-call(bf16[8,16,512]{2,1,0:T(8,128)(2,1)S(1)} %all_to_all.22.terms_ref), custom_call_target="tpu_custom_call" | custom-call | tf_op jit(solution)/shard_map/middle/pallas_call | solution.py:231
  51.7 4.9 %all-to-all-start.3 = ((bf16[16,16,512]{2,1,0:T(8,128)(2,1)}), bf16[16,16,512]{2,1,0:T(8,128)(2,1)S(1)}, u32[]{:S(2)}, u32[]{:S(2)}) async-start(bf16[16,16,512]{2,1,0:T(8,128)(2,1)} %middle.1), calls=%async_computation.3 | async-start | bytes 524288 | tf_op jit(solution)/shard_map/all_to_all | solution.py:246
  56.6 0.0 copy-start.2
  56.6 3.9 %update.1 = f32[8,2,256,256]{3,2,1,0:T(8,128)} custom-call(f32[2]{0:T(128)S(1)} %copy-done.3, f32[8,512]{1,0:T(8,128)S(1)} %get-tuple-element.12.keys_ref, f32[8,512]{1,0:T(8,128)S(1)} %get-tuple-element.13.values_ref, f32[8,2,256,256]{3,2,1,0:T(8,128)} %state_ref.5), custom_call_target="tpu_custom_call" | custom-call | flops 4194304 | bytes 8388608 | tf_op jit(solution)/shard_map/update/pallas_call | solution.py:206
  60.6 3.6 %all-to-all-done.3.terms_ref = bf16[16,16,512]{2,1,0:T(8,128)(2,1)S(1)} async-done(((bf16[16,16,512]{2,1,0:T(8,128)(2,1)}), bf16[16,16,512]{2,1,0:T(8,128)(2,1)S(1)}, u32[]{:S(2)}, u32[]{:S(2)}) %all-to-all-start.3) | async-done | bytes 262176 | tf_op jit(solution)/shard_map/all_to_all | solution.py:246
  64.2 0.0 copy-done.2
  64.2 0.7 %finish.1 = bf16[128,512]{1,0:T(8,128)(2,1)} custom-call(bf16[128,512]{1,0:T(8,128)(2,1)S(1)} %copy-done.2, bf16[16,16,512]{2,1,0:T(8,128)(2,1)S(1)} %all-to-all-done.3.terms_ref), custom_call_target="tpu_custom_call" | custom-call | tf_op jit(solution)/shard_map/finish/pallas_call | solution.py:239
  (1 shorter events, 0.0 us)
Async XLA Ops:
  0.6 1.7 %copy-start = (bf16[512,4,512]{2,1,0:T(4,128)(2,1)S(1)}, bf16[512,4,512]{2,1,0:T(4,128)(2,1)}, u32[]{:S(2)}) copy-start(bf16[512,4,512]{2,1,0:T(4,128)(2,1)} %param.8) | copy-start | bytes 6291460
  0.6 7.0 %copy-start.1 = (f32[8,2,256,256]{3,2,1,0:T(8,128)S(1)}, f32[8,2,256,256]{3,2,1,0:T(8,128)}, u32[]{:S(2)}) copy-start(f32[8,2,256,256]{3,2,1,0:T(8,128)} %state_ref.5) | copy-start | bytes 12582916
  3.1 4.5 %collective-permute-start = (bf16[4,64,512]{2,1,0:T(8,128)(2,1)S(1)}, bf16[4,64,512]{2,1,0:T(8,128)(2,1)S(1)}, u32[]{:S(2)}, u32[]{:S(2)}) collective-permute-start(bf16[4,64,512]{2,1,0:T(8,128)(2,1)S(1)} %slice.4), channel_id=1, source_target_pairs={{0,16},{16,0},{32,48},{48,32},{64,80},{80,64},{96,112},{112,96},{1... | collective-permute-start | bytes 786440 | tf_op jit(solution)/shard_map/ppermute | solution.py:180
  6.4 1.2 %collective-permute-start.1 = (f32[64,128]{1,0:T(8,128)S(1)}, f32[64,128]{1,0:T(8,128)S(1)}, u32[]{:S(2)}, u32[]{:S(2)}) collective-permute-start(f32[64,128]{1,0:T(8,128)S(1)} %get-tuple-element.10), channel_id=1, source_target_pairs={{0,16},{16,0},{32,48},{48,32},{64,80},{80,64},{96,112},{112,96},{1... | collective-permute-start | bytes 98312 | tf_op jit(solution)/shard_map/ppermute | solution.py:179
  7.6 18.2 %copy-start.3 = (f32[2]{0:T(128)S(1)}, f32[2]{0:T(128)}, u32[]{:S(2)}) copy-start(f32[2]{0:T(128)} %decay_ref.3) | copy-start | bytes 28
  25.8 14.7 %copy-start.4 = (bf16[512,512]{1,0:T(8,128)(2,1)S(1)}, bf16[512,512]{1,0:T(8,128)(2,1)}, u32[]{:S(2)}) copy-start(bf16[512,512]{1,0:T(8,128)(2,1)} %param.9) | copy-start | bytes 1572868
  51.7 12.4 %all-to-all-start.3 = ((bf16[16,16,512]{2,1,0:T(8,128)(2,1)}), bf16[16,16,512]{2,1,0:T(8,128)(2,1)S(1)}, u32[]{:S(2)}, u32[]{:S(2)}) async-start(bf16[16,16,512]{2,1,0:T(8,128)(2,1)} %middle.1), calls=%async_computation.3 | async-start | bytes 524288 | tf_op jit(solution)/shard_map/all_to_all | solution.py:246
  56.6 7.5 %copy-start.2 = (bf16[128,512]{1,0:T(8,128)(2,1)S(1)}, bf16[128,512]{1,0:T(8,128)(2,1)}, u32[]{:S(2)}) copy-start(bf16[128,512]{1,0:T(8,128)(2,1)} %tokens_ref.1) | copy-start | bytes 393220

commit v5 on v4

--- a/solution.py
+++ b/solution.py
@@ -85,7 +85,7 @@
         here = slice(h * HS, (h + 1) * HS)
         overlap = jnp.sum(queries[:, here] * keys[:, here], axis=1, keepdims=True)
         readout = (
-            decay_ref[h] * scale * jnp.concatenate(from_state[h], axis=0)
+            decay_ref[:, h : h + 1] * scale * jnp.concatenate(from_state[h], axis=0)
             + overlap * values[:, here]
         )
         centre = jnp.mean(readout, axis=1, keepdims=True)
@@ -197,12 +197,12 @@
             jax.ShapeDtypeStruct((own_rows, heads * HS), jnp.float32),
             jax.ShapeDtypeStruct((own_rows, heads * HS), jnp.float32),
         ),
-        in_specs=[smem, vmem, vmem],
+        in_specs=[vmem, vmem, vmem],
         out_specs=(vmem, vmem, vmem),
         scratch_shapes=[pltpu.VMEM((heads * HS, own_rows), jnp.float32)],
         compiler_params=pltpu.CompilerParams(vmem_limit_bytes=24 * 2**20),
         name="readout",
-    )(decay, parts, state)
+    )(decay.reshape(1, heads), parts, state)
     new_state = pl.pallas_call(
         update_kernel,
         out_shape=jax.ShapeDtypeStruct(state.shape, jnp.float32),

time: 65.4 us -> 64.9 us (level)
  no operation moved by 1% of the time
where the time goes in v5:
time: 64.9 us; the launch traced here: 64.4 us
  blocking collectives  41.3 us (64%)
  starting transfers between devices  8.3 us (13%)
  Pallas kernels  7.84 us (12%)
  waiting for transfers between devices  4.71 us (7%)
  matrix products  0.98 us (2%)
  between operations  0.72 us (1%)
    all_to_all x1, blocking collectives, local(): lax.all_to_all(pair.reshape(chips, own_rows, -1), 'gx', 0, 0, axis_index_...  18.1 us
    all_to_all x1, blocking collectives, local(): all_gated = lax.all_to_all(copies, 'gx', 0, 0).reshape(all_rows, -1)  13 us
    all_to_all x1, blocking collectives, local(): lax.all_to_all(head_terms.astype(jnp.bfloat16).reshape(blocks, all_rows /...  10.3 us
    all_to_all x1, starting transfers between devices, local(): lax.all_to_all(copies, 'gy', 0, 0)  4.87 us
    pallas_call x1, Pallas kernels, local(): pl.pallas_call(update_kernel, out_shape=jax.ShapeDtypeStruct(state.shape,...  3.92 us
    all_to_all x1, waiting for transfers between devices, local(): lax.all_to_all(copies, 'gy', 0, 0)  3.6 us
    ppermute x1, starting transfers between devices, local(): arrived = lax.ppermute(products[:, :half], 'gx', swap)  3.33 us
  transfers between devices with their start and end apart: 3, of which 2 were waited for; matrix products, arithmetic and copies ran while one was open for 0% of the time, Pallas kernels for 6%

profile of v5, /device:TPU:1, one launch (start us, length us, event | category | flops | bytes accessed | tf_op | source)
XLA Modules:
  0.0 64.4 jit_solution(15368457157399709430)
XLA Ops:
  0.6 0.0 copy-start
  0.6 0.0 copy-start.1
  0.7 1.2 %scale.1 = (bf16[4,128,512]{2,1,0:T(8,128)(2,1)S(1)}, f32[64,128]{1,0:T(8,128)S(1)}, f32[64,128]{1,0:T(8,128)S(1)}) custom-call(bf16[128,512]{1,0:T(8,128)(2,1)} %tokens_ref.1, f32[1,512]{1,0:T(1,128)} %bitcast.12), custom_call_target="tpu_custom_call" | custom-call | flops 8589934592 | bytes 262144 | tf_op jit(solution)/shard_map/scale/pallas_call | solution.py:151
  1.9 0.4 copy-done
  2.3 0.8 %fusion.2.products_ref = bf16[4,128,512]{2,1,0:T(8,128)(2,1)S(1)} fusion(bf16[4,128,512]{2,1,0:T(8,128)(2,1)S(1)} %get-tuple-element.8, bf16[512,4,512]{2,1,0:T(4,128)(2,1)S(1)} %copy-done), kind=kOutput, calls=%fused_computation.2 | convolution fusion | flops 268697600 | bytes 3145728 | tf_op jit(solution)/shard_map/psi,ipo->pso/dot_general | solution.py:174
  3.1 3.3 %collective-permute-start = (bf16[4,64,512]{2,1,0:T(8,128)(2,1)S(1)}, bf16[4,64,512]{2,1,0:T(8,128)(2,1)S(1)}, u32[]{:S(2)}, u32[]{:S(2)}) collective-permute-start(bf16[4,64,512]{2,1,0:T(8,128)(2,1)S(1)} %slice.4), channel_id=1, source_target_pairs={{0,16},{16,0},{32,48},{48,32},{64,80},{80,64},{96,112},{112,96},{1... | collective-permute-start | bytes 786440 | tf_op jit(solution)/shard_map/ppermute | solution.py:180
  6.4 0.1 collective-permute-start.1
  6.5 1.1 %collective-permute-done.1.other_ref = f32[64,128]{1,0:T(8,128)S(1)} collective-permute-done((f32[64,128]{1,0:T(8,128)S(1)}, f32[64,128]{1,0:T(8,128)S(1)}, u32[]{:S(2)}, u32[]{:S(2)}) %collective-permute-start.1) | collective-permute-done | bytes 32800 | tf_op jit(solution)/shard_map/ppermute | solution.py:179
  7.6 0.0 collective-permute-done.arrived_ref
  7.6 0.0 copy-done.1
  7.6 0.0 copy-start.3
  7.6 0.1 pair.1
  7.7 18.1 %all_to_all.20.parts_ref = bf16[8,8,2176]{2,1,0:T(8,128)(2,1)S(1)} all-to-all(bf16[8,8,2176]{2,1,0:T(8,128)(2,1)S(1)} %bitcast.9), channel_id=1, replica_groups={{0,32,64,96,128,160,192,224},{16,48,80,112,144,176,208,240},{1,33,65,97..., dimensions={0} | all-to-all | bytes 557056 | tf_op jit(solution)/shard_map/all_to_all | solution.py:190
  25.8 0.0 copy-done.3
  25.8 0.0 copy-start.4
  25.8 1.2 %readout.1 = (bf16[16,8,512]{2,1,0:T(8,128)(2,1)S(1)}, f32[8,512]{1,0:T(8,128)S(1)}, f32[8,512]{1,0:T(8,128)S(1)}) custom-call(f32[1,2]{1,0:T(1,128)S(1)} %bitcast.10, bf16[8,8,2176]{2,1,0:T(8,128)(2,1)S(1)} %all_to_all.20.parts_ref, f32[8,2,256,256]{3,2,1,0:T(8,128)S(1)} %copy-done.1), custom_call_target="tpu_custom_call" | custom-call | tf_op jit(solution)/shard_map/readout/pallas_call | solution.py:193
  27.0 13.0 %all_to_all.21 = bf16[16,8,512]{2,1,0:T(8,128)(2,1)S(1)} all-to-all(bf16[16,8,512]{2,1,0:T(8,128)(2,1)S(1)} %get-tuple-element.11), channel_id=1, replica_groups=mesh['gx'=16,'gy'=16] {'gx'}, dimensions={0} | all-to-all | bytes 262144 | tf_op jit(solution)/shard_map/all_to_all | solution.py:222
  39.9 0.0 copy-done.4
  40.0 0.2 convolution_convert_fusion
  40.2 10.3 %all_to_all.22.terms_ref = bf16[8,16,512]{2,1,0:T(8,128)(2,1)S(1)} all-to-all(bf16[8,16,512]{2,1,0:T(8,128)(2,1)S(1)} %bitcast.11), channel_id=1, replica_groups={{0,1,2,3,4,5,6,7},{8,9,10,11,12,13,14,15},{16,17,18,19,20,21,22,23},{24..., dimensions={0} | all-to-all | bytes 262144 | tf_op jit(solution)/shard_map/all_to_all | solution.py:227
  50.5 0.7 %middle.1 = bf16[16,16,512]{2,1,0:T(8,128)(2,1)} custom-call(bf16[8,16,512]{2,1,0:T(8,128)(2,1)S(1)} %all_to_all.22.terms_ref), custom_call_target="tpu_custom_call" | custom-call | tf_op jit(solution)/shard_map/middle/pallas_call | solution.py:231
  51.2 4.9 %all-to-all-start.3 = ((bf16[16,16,512]{2,1,0:T(8,128)(2,1)}), bf16[16,16,512]{2,1,0:T(8,128)(2,1)S(1)}, u32[]{:S(2)}, u32[]{:S(2)}) async-start(bf16[16,16,512]{2,1,0:T(8,128)(2,1)} %middle.1), calls=%async_computation.3 | async-start | bytes 524288 | tf_op jit(solution)/shard_map/all_to_all | solution.py:246
  56.1 0.0 copy-start.2
  56.1 3.9 %update.1 = f32[8,2,256,256]{3,2,1,0:T(8,128)} custom-call(f32[2]{0:T(128)S(1)} %copy-done.3, f32[8,512]{1,0:T(8,128)S(1)} %get-tuple-element.12.keys_ref, f32[8,512]{1,0:T(8,128)S(1)} %get-tuple-element.13.values_ref, f32[8,2,256,256]{3,2,1,0:T(8,128)} %state_ref.5), custom_call_target="tpu_custom_call" | custom-call | flops 4194304 | bytes 8388608 | tf_op jit(solution)/shard_map/update/pallas_call | solution.py:206
  60.1 3.6 %all-to-all-done.3.terms_ref = bf16[16,16,512]{2,1,0:T(8,128)(2,1)S(1)} async-done(((bf16[16,16,512]{2,1,0:T(8,128)(2,1)}), bf16[16,16,512]{2,1,0:T(8,128)(2,1)S(1)}, u32[]{:S(2)}, u32[]{:S(2)}) %all-to-all-start.3) | async-done | bytes 262176 | tf_op jit(solution)/shard_map/all_to_all | solution.py:246
  63.7 0.0 copy-done.2
  63.7 0.7 %finish.1 = bf16[128,512]{1,0:T(8,128)(2,1)} custom-call(bf16[128,512]{1,0:T(8,128)(2,1)S(1)} %copy-done.2, bf16[16,16,512]{2,1,0:T(8,128)(2,1)S(1)} %all-to-all-done.3.terms_ref), custom_call_target="tpu_custom_call" | custom-call | tf_op jit(solution)/shard_map/finish/pallas_call | solution.py:239
  (1 shorter events, 0.0 us)
Async XLA Ops:
  0.6 1.7 %copy-start = (bf16[512,4,512]{2,1,0:T(4,128)(2,1)S(1)}, bf16[512,4,512]{2,1,0:T(4,128)(2,1)}, u32[]{:S(2)}) copy-start(bf16[512,4,512]{2,1,0:T(4,128)(2,1)} %param.8) | copy-start | bytes 6291460
  0.6 7.0 %copy-start.1 = (f32[8,2,256,256]{3,2,1,0:T(8,128)S(1)}, f32[8,2,256,256]{3,2,1,0:T(8,128)}, u32[]{:S(2)}) copy-start(f32[8,2,256,256]{3,2,1,0:T(8,128)} %state_ref.5) | copy-start | bytes 12582916
  3.1 4.5 %collective-permute-start = (bf16[4,64,512]{2,1,0:T(8,128)(2,1)S(1)}, bf16[4,64,512]{2,1,0:T(8,128)(2,1)S(1)}, u32[]{:S(2)}, u32[]{:S(2)}) collective-permute-start(bf16[4,64,512]{2,1,0:T(8,128)(2,1)S(1)} %slice.4), channel_id=1, source_target_pairs={{0,16},{16,0},{32,48},{48,32},{64,80},{80,64},{96,112},{112,96},{1... | collective-permute-start | bytes 786440 | tf_op jit(solution)/shard_map/ppermute | solution.py:180
  6.4 1.2 %collective-permute-start.1 = (f32[64,128]{1,0:T(8,128)S(1)}, f32[64,128]{1,0:T(8,128)S(1)}, u32[]{:S(2)}, u32[]{:S(2)}) collective-permute-start(f32[64,128]{1,0:T(8,128)S(1)} %get-tuple-element.10), channel_id=1, source_target_pairs={{0,16},{16,0},{32,48},{48,32},{64,80},{80,64},{96,112},{112,96},{1... | collective-permute-start | bytes 98312 | tf_op jit(solution)/shard_map/ppermute | solution.py:179
  7.6 18.2 %copy-start.3 = (f32[2]{0:T(128)S(1)}, f32[2]{0:T(128)}, u32[]{:S(2)}) copy-start(f32[2]{0:T(128)} %decay_ref.1) | copy-start | bytes 28
  25.8 14.2 %copy-start.4 = (bf16[512,512]{1,0:T(8,128)(2,1)S(1)}, bf16[512,512]{1,0:T(8,128)(2,1)}, u32[]{:S(2)}) copy-start(bf16[512,512]{1,0:T(8,128)(2,1)} %param.9) | copy-start | bytes 1572868
  51.2 12.4 %all-to-all-start.3 = ((bf16[16,16,512]{2,1,0:T(8,128)(2,1)}), bf16[16,16,512]{2,1,0:T(8,128)(2,1)S(1)}, u32[]{:S(2)}, u32[]{:S(2)}) async-start(bf16[16,16,512]{2,1,0:T(8,128)(2,1)} %middle.1), calls=%async_computation.3 | async-start | bytes 524288 | tf_op jit(solution)/shard_map/all_to_all | solution.py:246
  56.1 7.5 %copy-start.2 = (bf16[128,512]{1,0:T(8,128)(2,1)S(1)}, bf16[128,512]{1,0:T(8,128)(2,1)}, u32[]{:S(2)}) copy-start(bf16[128,512]{1,0:T(8,128)(2,1)} %tokens_ref.1) | copy-start | bytes 393220

commit v6 on v5

--- a/solution.py
+++ b/solution.py
@@ -128,17 +128,19 @@
 
 
 def finish_kernel(tokens_ref, terms_ref, mixed_ref):
-    blocks, rows, _ = terms_ref.shape
-    blocks //= 2
-    for n in range(blocks):
-        here = slice(n * rows, (n + 1) * rows)
-        total = terms_ref[n].astype(jnp.float32) + terms_ref[blocks + n].astype(jnp.float32)
-        mixed_ref[here] = (tokens_ref[here].astype(jnp.float32) + total).astype(jnp.bfloat16)
+    rows = terms_ref.shape[1]
+    for y in range(2):
+        for x in range(2):
+            n = 2 * y + x
+            here = slice(n * rows, (n + 1) * rows)
+            total = terms_ref[4 * y + x].astype(jnp.float32)
+            total += terms_ref[4 * y + 2 + x].astype(jnp.float32)
+            mixed_ref[here] = (tokens_ref[here].astype(jnp.float32) + total).astype(jnp.bfloat16)
 
 
 def local(tokens, norm_gain, w_project, w_output, decay, state):
     all_rows, features = tokens.shape
-    size_x, size_y = lax.axis_size("gx"), lax.axis_size("gy")
+    size_x = lax.axis_size("gx")
     chips = size_x // 2
     own_rows = all_rows // size_x
     heads = state.shape[1]
@@ -221,16 +223,15 @@
     )(decay, keys, values, state_hbm)
     all_gated = lax.all_to_all(copies, "gx", 0, 0).reshape(all_rows, -1)
     head_terms = jnp.dot(all_gated, w_output, preferred_element_type=jnp.float32)
-    blocks = size_y // 2
-    halves = [list(range(blocks)), list(range(blocks, size_y))]
+    by_x = [[4 * y + 2 * h + x for y in range(4) for x in range(2)] for h in range(2)]
+    by_y = [[4 * (2 * h + y) + x for y in range(2) for x in range(4)] for h in range(2)]
     params = pltpu.CompilerParams(vmem_limit_bytes=16 * 2**20)
-    terms = lax.all_to_all(
-        head_terms.astype(jnp.bfloat16).reshape(blocks, all_rows // blocks, features),
-        "gy", 0, 0, axis_index_groups=halves,
-    )
+    pieces = head_terms.astype(jnp.bfloat16).reshape(1, 4, all_rows // 4, features)
+    pieces = jnp.broadcast_to(pieces, (2,) + pieces.shape[1:]).reshape((8,) + pieces.shape[2:])
+    terms = lax.all_to_all(pieces, "gy", 0, 0, axis_index_groups=by_x)
     copies = pl.pallas_call(
         middle_kernel,
-        out_shape=jax.ShapeDtypeStruct((size_y,) + terms.shape[1:], jnp.bfloat16),
+        out_shape=jax.ShapeDtypeStruct(terms.shape, jnp.bfloat16),
         in_specs=[vmem],
         out_specs=vmem,
         compiler_params=params,
@@ -243,7 +244,7 @@
         out_specs=vmem,
         compiler_params=params,
         name="finish",
-    )(tokens, lax.all_to_all(copies, "gy", 0, 0))
+    )(tokens, lax.all_to_all(copies, "gy", 0, 0, axis_index_groups=by_y))
     return (mixed, new_state)
 
 

time: 64.9 us -> 64.3 us (level)
  blocking collectives: 41.3 us -> 43.1 us
  starting transfers between devices: 8.3 us -> 7.15 us
  waiting for transfers between devices: 4.71 us -> 3.66 us
    all_to_all x1, blocking collectives: 10.3 us -> 12.1 us  [local(): terms = lax.all_to_all(pieces, 'gy', 0, 0, axis_index_groups=by_x)]
    all_to_all x1, starting transfers between devices: 4.87 us -> 3.73 us  [local(): lax.all_to_all(copies, 'gy', 0, 0, axis_index_groups=by_y)]
    all_to_all x1, waiting for transfers between devices: 3.6 us -> 2.55 us  [local(): lax.all_to_all(copies, 'gy', 0, 0, axis_index_groups=by_y)]
where the time goes in v6:
time: 64.3 us; the launch traced here: 64 us
  blocking collectives  43.1 us (67%)
  Pallas kernels  7.85 us (12%)
  starting transfers between devices  7.15 us (11%)
  waiting for transfers between devices  3.66 us (6%)
  matrix products  0.98 us (2%)
  between operations  0.72 us (1%)
    all_to_all x1, blocking collectives, local(): lax.all_to_all(pair.reshape(chips, own_rows, -1), 'gx', 0, 0, axis_index_...  18.1 us
    all_to_all x1, blocking collectives, local(): all_gated = lax.all_to_all(copies, 'gx', 0, 0).reshape(all_rows, -1)  13 us
    all_to_all x1, blocking collectives, local(): terms = lax.all_to_all(pieces, 'gy', 0, 0, axis_index_groups=by_x)  12.1 us
    pallas_call x1, Pallas kernels, local(): pl.pallas_call(update_kernel, out_shape=jax.ShapeDtypeStruct(state.shape,...  3.92 us
    all_to_all x1, starting transfers between devices, local(): lax.all_to_all(copies, 'gy', 0, 0, axis_index_groups=by_y)  3.73 us
    ppermute x1, starting transfers between devices, local(): arrived = lax.ppermute(products[:, :half], 'gx', swap)  3.33 us
    all_to_all x1, waiting for transfers between devices, local(): lax.all_to_all(copies, 'gy', 0, 0, axis_index_groups=by_y)  2.55 us
  transfers between devices with their start and end apart: 3, of which 2 were waited for; matrix products, arithmetic and copies ran while one was open for 0% of the time, Pallas kernels for 6%

profile of v6, /device:TPU:1, one launch (start us, length us, event | category | flops | bytes accessed | tf_op | source)
XLA Modules:
  0.0 64.0 jit_solution(13566781600894713314)
XLA Ops:
  0.6 0.0 copy-start
  0.6 0.0 copy-start.1
  0.7 1.2 %scale.1 = (bf16[4,128,512]{2,1,0:T(8,128)(2,1)S(1)}, f32[64,128]{1,0:T(8,128)S(1)}, f32[64,128]{1,0:T(8,128)S(1)}) custom-call(bf16[128,512]{1,0:T(8,128)(2,1)} %tokens_ref.1, f32[1,512]{1,0:T(1,128)} %bitcast.14), custom_call_target="tpu_custom_call" | custom-call | flops 8589934592 | bytes 262144 | tf_op jit(solution)/shard_map/scale/pallas_call | solution.py:153
  1.9 0.4 copy-done
  2.3 0.8 %fusion.2.products_ref = bf16[4,128,512]{2,1,0:T(8,128)(2,1)S(1)} fusion(bf16[4,128,512]{2,1,0:T(8,128)(2,1)S(1)} %get-tuple-element.8, bf16[512,4,512]{2,1,0:T(4,128)(2,1)S(1)} %copy-done), kind=kOutput, calls=%fused_computation.2 | convolution fusion | flops 268697600 | bytes 3145728 | tf_op jit(solution)/shard_map/psi,ipo->pso/dot_general | solution.py:176
  3.1 3.3 %collective-permute-start = (bf16[4,64,512]{2,1,0:T(8,128)(2,1)S(1)}, bf16[4,64,512]{2,1,0:T(8,128)(2,1)S(1)}, u32[]{:S(2)}, u32[]{:S(2)}) collective-permute-start(bf16[4,64,512]{2,1,0:T(8,128)(2,1)S(1)} %slice.4), channel_id=1, source_target_pairs={{0,16},{16,0},{32,48},{48,32},{64,80},{80,64},{96,112},{112,96},{1... | collective-permute-start | bytes 786440 | tf_op jit(solution)/shard_map/ppermute | solution.py:182
  6.4 0.1 collective-permute-start.1
  6.5 1.1 %collective-permute-done.1.other_ref = f32[64,128]{1,0:T(8,128)S(1)} collective-permute-done((f32[64,128]{1,0:T(8,128)S(1)}, f32[64,128]{1,0:T(8,128)S(1)}, u32[]{:S(2)}, u32[]{:S(2)}) %collective-permute-start.1) | collective-permute-done | bytes 32800 | tf_op jit(solution)/shard_map/ppermute | solution.py:181
  7.6 0.0 collective-permute-done.arrived_ref
  7.6 0.0 copy-done.1
  7.6 0.0 copy-start.3
  7.6 0.1 pair.1
  7.7 18.1 %all_to_all.20.parts_ref = bf16[8,8,2176]{2,1,0:T(8,128)(2,1)S(1)} all-to-all(bf16[8,8,2176]{2,1,0:T(8,128)(2,1)S(1)} %bitcast.10), channel_id=1, replica_groups={{0,32,64,96,128,160,192,224},{16,48,80,112,144,176,208,240},{1,33,65,97..., dimensions={0} | all-to-all | bytes 557056 | tf_op jit(solution)/shard_map/all_to_all | solution.py:192
  25.8 0.0 copy-done.3
  25.8 0.0 copy-start.4
  25.8 1.2 %readout.1 = (bf16[16,8,512]{2,1,0:T(8,128)(2,1)S(1)}, f32[8,512]{1,0:T(8,128)S(1)}, f32[8,512]{1,0:T(8,128)S(1)}) custom-call(f32[1,2]{1,0:T(1,128)S(1)} %bitcast.11, bf16[8,8,2176]{2,1,0:T(8,128)(2,1)S(1)} %all_to_all.20.parts_ref, f32[8,2,256,256]{3,2,1,0:T(8,128)S(1)} %copy-done.1), custom_call_target="tpu_custom_call" | custom-call | tf_op jit(solution)/shard_map/readout/pallas_call | solution.py:195
  27.0 13.0 %all_to_all.21 = bf16[16,8,512]{2,1,0:T(8,128)(2,1)S(1)} all-to-all(bf16[16,8,512]{2,1,0:T(8,128)(2,1)S(1)} %get-tuple-element.11), channel_id=1, replica_groups=mesh['gx'=16,'gy'=16] {'gx'}, dimensions={0} | all-to-all | bytes 262144 | tf_op jit(solution)/shard_map/all_to_all | solution.py:224
  39.9 0.0 copy-done.4
  40.0 0.2 convolution_convert_fusion
  40.2 12.1 %all_to_all.22.terms_ref = bf16[8,32,512]{2,1,0:T(8,128)(2,1)S(1)} all-to-all(bf16[8,32,512]{2,1,0:T(8,128)(2,1)S(1)} %bitcast.12), channel_id=1, replica_groups={{0,1,4,5,8,9,12,13},{2,3,6,7,10,11,14,15},{16,17,20,21,24,25,28,29},{18..., dimensions={0} | all-to-all | bytes 524288 | tf_op jit(solution)/shard_map/all_to_all | solution.py:231
  52.3 0.8 %middle.1 = bf16[8,32,512]{2,1,0:T(8,128)(2,1)} custom-call(bf16[8,32,512]{2,1,0:T(8,128)(2,1)S(1)} %all_to_all.22.terms_ref), custom_call_target="tpu_custom_call" | custom-call | tf_op jit(solution)/shard_map/middle/pallas_call | solution.py:232
  53.1 3.7 %all-to-all-start.3 = ((bf16[8,32,512]{2,1,0:T(8,128)(2,1)}), bf16[8,32,512]{2,1,0:T(8,128)(2,1)S(1)}, u32[]{:S(2)}, u32[]{:S(2)}) async-start(bf16[8,32,512]{2,1,0:T(8,128)(2,1)} %middle.1), calls=%async_computation.3 | async-start | bytes 524288 | tf_op jit(solution)/shard_map/all_to_all | solution.py:247
  56.8 0.0 copy-start.2
  56.8 3.9 %update.1 = f32[8,2,256,256]{3,2,1,0:T(8,128)} custom-call(f32[2]{0:T(128)S(1)} %copy-done.3, f32[8,512]{1,0:T(8,128)S(1)} %get-tuple-element.12.keys_ref, f32[8,512]{1,0:T(8,128)S(1)} %get-tuple-element.13.values_ref, f32[8,2,256,256]{3,2,1,0:T(8,128)} %state_ref.5), custom_call_target="tpu_custom_call" | custom-call | flops 4194304 | bytes 8388608 | tf_op jit(solution)/shard_map/update/pallas_call | solution.py:208
  60.7 2.6 %all-to-all-done.3.terms_ref = bf16[8,32,512]{2,1,0:T(8,128)(2,1)S(1)} async-done(((bf16[8,32,512]{2,1,0:T(8,128)(2,1)}), bf16[8,32,512]{2,1,0:T(8,128)(2,1)S(1)}, u32[]{:S(2)}, u32[]{:S(2)}) %all-to-all-start.3) | async-done | bytes 262176 | tf_op jit(solution)/shard_map/all_to_all | solution.py:247
  63.3 0.0 copy-done.2
  63.3 0.7 %finish.1 = bf16[128,512]{1,0:T(8,128)(2,1)} custom-call(bf16[128,512]{1,0:T(8,128)(2,1)S(1)} %copy-done.2, bf16[8,32,512]{2,1,0:T(8,128)(2,1)S(1)} %all-to-all-done.3.terms_ref), custom_call_target="tpu_custom_call" | custom-call | tf_op jit(solution)/shard_map/finish/pallas_call | solution.py:240
  (2 shorter events, 0.0 us)
Async XLA Ops:
  0.6 1.7 %copy-start = (bf16[512,4,512]{2,1,0:T(4,128)(2,1)S(1)}, bf16[512,4,512]{2,1,0:T(4,128)(2,1)}, u32[]{:S(2)}) copy-start(bf16[512,4,512]{2,1,0:T(4,128)(2,1)} %param.8) | copy-start | bytes 6291460
  0.6 7.0 %copy-start.1 = (f32[8,2,256,256]{3,2,1,0:T(8,128)S(1)}, f32[8,2,256,256]{3,2,1,0:T(8,128)}, u32[]{:S(2)}) copy-start(f32[8,2,256,256]{3,2,1,0:T(8,128)} %state_ref.5) | copy-start | bytes 12582916
  3.1 4.5 %collective-permute-start = (bf16[4,64,512]{2,1,0:T(8,128)(2,1)S(1)}, bf16[4,64,512]{2,1,0:T(8,128)(2,1)S(1)}, u32[]{:S(2)}, u32[]{:S(2)}) collective-permute-start(bf16[4,64,512]{2,1,0:T(8,128)(2,1)S(1)} %slice.4), channel_id=1, source_target_pairs={{0,16},{16,0},{32,48},{48,32},{64,80},{80,64},{96,112},{112,96},{1... | collective-permute-start | bytes 786440 | tf_op jit(solution)/shard_map/ppermute | solution.py:182
  6.4 1.2 %collective-permute-start.1 = (f32[64,128]{1,0:T(8,128)S(1)}, f32[64,128]{1,0:T(8,128)S(1)}, u32[]{:S(2)}, u32[]{:S(2)}) collective-permute-start(f32[64,128]{1,0:T(8,128)S(1)} %get-tuple-element.10), channel_id=1, source_target_pairs={{0,16},{16,0},{32,48},{48,32},{64,80},{80,64},{96,112},{112,96},{1... | collective-permute-start | bytes 98312 | tf_op jit(solution)/shard_map/ppermute | solution.py:181
  7.6 18.2 %copy-start.3 = (f32[2]{0:T(128)S(1)}, f32[2]{0:T(128)}, u32[]{:S(2)}) copy-start(f32[2]{0:T(128)} %decay_ref.1) | copy-start | bytes 28
  25.8 14.2 %copy-start.4 = (bf16[512,512]{1,0:T(8,128)(2,1)S(1)}, bf16[512,512]{1,0:T(8,128)(2,1)}, u32[]{:S(2)}) copy-start(bf16[512,512]{1,0:T(8,128)(2,1)} %param.9) | copy-start | bytes 1572868
  53.1 10.2 %all-to-all-start.3 = ((bf16[8,32,512]{2,1,0:T(8,128)(2,1)}), bf16[8,32,512]{2,1,0:T(8,128)(2,1)S(1)}, u32[]{:S(2)}, u32[]{:S(2)}) async-start(bf16[8,32,512]{2,1,0:T(8,128)(2,1)} %middle.1), calls=%async_computation.3 | async-start | bytes 524288 | tf_op jit(solution)/shard_map/all_to_all | solution.py:247
  56.8 6.5 %copy-start.2 = (bf16[128,512]{1,0:T(8,128)(2,1)S(1)}, bf16[128,512]{1,0:T(8,128)(2,1)}, u32[]{:S(2)}) copy-start(bf16[128,512]{1,0:T(8,128)(2,1)} %tokens_ref.1) | copy-start | bytes 393220

commit v7 on v6

--- a/solution.py
+++ b/solution.py
@@ -114,7 +114,8 @@
         for h in range(heads):
             key_col = key_cols_ref[h * HS : (h + 1) * HS, s : s + 1]
             value_row = values_ref[s : s + 1, h * HS : (h + 1) * HS]
-            fresh_ref[s, h] = decay_ref[h] * held_ref[s, h] + key_col * value_row
+            decay = decay_ref[:, h : h + 1]
+            fresh_ref[s, h] = decay * held_ref[s, h] + key_col * value_row
         stores[s].start()
     for store in stores:
         store.wait()
@@ -148,7 +149,6 @@
     padded = kinds * width + LANES
     half = all_rows // 2
     vmem = pl.BlockSpec(memory_space=pltpu.VMEM)
-    smem = pl.BlockSpec(memory_space=pltpu.SMEM)
     hbm = pl.BlockSpec(memory_space=pltpu.HBM)
     scaled, away_squares, own_squares = pl.pallas_call(
         scale_kernel,
@@ -208,7 +208,7 @@
     new_state = pl.pallas_call(
         update_kernel,
         out_shape=jax.ShapeDtypeStruct(state.shape, jnp.float32),
-        in_specs=[smem, vmem, vmem, hbm],
+        in_specs=[vmem, vmem, vmem, hbm],
         out_specs=hbm,
         scratch_shapes=[
             pltpu.VMEM((heads * HS, own_rows), jnp.float32),
@@ -220,7 +220,7 @@
         compiler_params=pltpu.CompilerParams(vmem_limit_bytes=24 * 2**20),
         cost_estimate=pl.CostEstimate(flops=2**22, bytes_accessed=2**23, transcendentals=0),
         name="update",
-    )(decay, keys, values, state_hbm)
+    )(decay.reshape(1, heads), keys, values, state_hbm)
     all_gated = lax.all_to_all(copies, "gx", 0, 0).reshape(all_rows, -1)
     head_terms = jnp.dot(all_gated, w_output, preferred_element_type=jnp.float32)
     by_x = [[4 * y + 2 * h + x for y in range(4) for x in range(2)] for h in range(2)]

time: 64.3 us -> 64.3 us (level)
  transfers between devices with their start and end apart: 3 -> 3, of which waited for: 2 -> 2; matrix products, arithmetic and copies ran while one was open for 0% -> 0% of each run, Pallas kernels for 6% -> 5%
where the time goes in v7:
time: 64.3 us; the launch traced here: 64 us
  blocking collectives  43.1 us (67%)
  Pallas kernels  7.35 us (11%)
  starting transfers between devices  7.15 us (11%)
  waiting for transfers between devices  4.16 us (6%)
  matrix products  0.98 us (2%)
  between operations  0.72 us (1%)
    all_to_all x1, blocking collectives, local(): lax.all_to_all(pair.reshape(chips, own_rows, -1), 'gx', 0, 0, axis_index_...  18.1 us
    all_to_all x1, blocking collectives, local(): all_gated = lax.all_to_all(copies, 'gx', 0, 0).reshape(all_rows, -1)  13 us
    all_to_all x1, blocking collectives, local(): terms = lax.all_to_all(pieces, 'gy', 0, 0, axis_index_groups=by_x)  12.1 us
    all_to_all x1, starting transfers between devices, local(): lax.all_to_all(copies, 'gy', 0, 0, axis_index_groups=by_y)  3.73 us
    pallas_call x1, Pallas kernels, local(): pl.pallas_call(update_kernel, out_shape=jax.ShapeDtypeStruct(state.shape,...  3.42 us
    ppermute x1, starting transfers between devices, local(): arrived = lax.ppermute(products[:, :half], 'gx', swap)  3.33 us
    all_to_all x1, waiting for transfers between devices, local(): lax.all_to_all(copies, 'gy', 0, 0, axis_index_groups=by_y)  3.05 us
  transfers between devices with their start and end apart: 3, of which 2 were waited for; matrix products, arithmetic and copies ran while one was open for 0% of the time, Pallas kernels for 5%

profile of v7, /device:TPU:1, one launch (start us, length us, event | category | flops | bytes accessed | tf_op | source)
XLA Modules:
  0.0 64.0 jit_solution(10958152641353921833)
XLA Ops:
  0.6 0.0 copy-start
  0.6 0.0 copy-start.1
  0.7 1.2 %scale.1 = (bf16[4,128,512]{2,1,0:T(8,128)(2,1)S(1)}, f32[64,128]{1,0:T(8,128)S(1)}, f32[64,128]{1,0:T(8,128)S(1)}) custom-call(bf16[128,512]{1,0:T(8,128)(2,1)} %tokens_ref.1, f32[1,512]{1,0:T(1,128)} %bitcast.15), custom_call_target="tpu_custom_call" | custom-call | flops 8589934592 | bytes 262144 | tf_op jit(solution)/shard_map/scale/pallas_call | solution.py:153
  1.9 0.4 copy-done
  2.3 0.8 %fusion.2.products_ref = bf16[4,128,512]{2,1,0:T(8,128)(2,1)S(1)} fusion(bf16[4,128,512]{2,1,0:T(8,128)(2,1)S(1)} %get-tuple-element.8, bf16[512,4,512]{2,1,0:T(4,128)(2,1)S(1)} %copy-done), kind=kOutput, calls=%fused_computation.2 | convolution fusion | flops 268697600 | bytes 3145728 | tf_op jit(solution)/shard_map/psi,ipo->pso/dot_general | solution.py:176
  3.1 3.3 %collective-permute-start = (bf16[4,64,512]{2,1,0:T(8,128)(2,1)S(1)}, bf16[4,64,512]{2,1,0:T(8,128)(2,1)S(1)}, u32[]{:S(2)}, u32[]{:S(2)}) collective-permute-start(bf16[4,64,512]{2,1,0:T(8,128)(2,1)S(1)} %slice.4), channel_id=1, source_target_pairs={{0,16},{16,0},{32,48},{48,32},{64,80},{80,64},{96,112},{112,96},{1... | collective-permute-start | bytes 786440 | tf_op jit(solution)/shard_map/ppermute | solution.py:182
  6.4 0.1 collective-permute-start.1
  6.5 1.1 %collective-permute-done.1.other_ref = f32[64,128]{1,0:T(8,128)S(1)} collective-permute-done((f32[64,128]{1,0:T(8,128)S(1)}, f32[64,128]{1,0:T(8,128)S(1)}, u32[]{:S(2)}, u32[]{:S(2)}) %collective-permute-start.1) | collective-permute-done | bytes 32800 | tf_op jit(solution)/shard_map/ppermute | solution.py:181
  7.6 0.0 collective-permute-done.arrived_ref
  7.6 0.0 copy-done.1
  7.6 0.0 copy-start.3
  7.6 0.1 pair.1
  7.7 18.1 %all_to_all.20.parts_ref = bf16[8,8,2176]{2,1,0:T(8,128)(2,1)S(1)} all-to-all(bf16[8,8,2176]{2,1,0:T(8,128)(2,1)S(1)} %bitcast.10), channel_id=1, replica_groups={{0,32,64,96,128,160,192,224},{16,48,80,112,144,176,208,240},{1,33,65,97..., dimensions={0} | all-to-all | bytes 557056 | tf_op jit(solution)/shard_map/all_to_all | solution.py:192
  25.8 0.0 copy-done.3
  25.8 0.0 copy-start.4
  25.8 1.2 %readout.1 = (bf16[16,8,512]{2,1,0:T(8,128)(2,1)S(1)}, f32[8,512]{1,0:T(8,128)S(1)}, f32[8,512]{1,0:T(8,128)S(1)}) custom-call(f32[1,2]{1,0:T(1,128)S(1)} %bitcast.11, bf16[8,8,2176]{2,1,0:T(8,128)(2,1)S(1)} %all_to_all.20.parts_ref, f32[8,2,256,256]{3,2,1,0:T(8,128)S(1)} %copy-done.1), custom_call_target="tpu_custom_call" | custom-call | tf_op jit(solution)/shard_map/readout/pallas_call | solution.py:195
  27.0 13.0 %all_to_all.21 = bf16[16,8,512]{2,1,0:T(8,128)(2,1)S(1)} all-to-all(bf16[16,8,512]{2,1,0:T(8,128)(2,1)S(1)} %get-tuple-element.11), channel_id=1, replica_groups=mesh['gx'=16,'gy'=16] {'gx'}, dimensions={0} | all-to-all | bytes 262144 | tf_op jit(solution)/shard_map/all_to_all | solution.py:224
  39.9 0.0 copy-done.4
  40.0 0.2 convolution_convert_fusion
  40.2 12.1 %all_to_all.22.terms_ref = bf16[8,32,512]{2,1,0:T(8,128)(2,1)S(1)} all-to-all(bf16[8,32,512]{2,1,0:T(8,128)(2,1)S(1)} %bitcast.13), channel_id=1, replica_groups={{0,1,4,5,8,9,12,13},{2,3,6,7,10,11,14,15},{16,17,20,21,24,25,28,29},{18..., dimensions={0} | all-to-all | bytes 524288 | tf_op jit(solution)/shard_map/all_to_all | solution.py:231
  52.3 0.8 %middle.1 = bf16[8,32,512]{2,1,0:T(8,128)(2,1)} custom-call(bf16[8,32,512]{2,1,0:T(8,128)(2,1)S(1)} %all_to_all.22.terms_ref), custom_call_target="tpu_custom_call" | custom-call | tf_op jit(solution)/shard_map/middle/pallas_call | solution.py:232
  53.1 3.7 %all-to-all-start.3 = ((bf16[8,32,512]{2,1,0:T(8,128)(2,1)}), bf16[8,32,512]{2,1,0:T(8,128)(2,1)S(1)}, u32[]{:S(2)}, u32[]{:S(2)}) async-start(bf16[8,32,512]{2,1,0:T(8,128)(2,1)} %middle.1), calls=%async_computation.3 | async-start | bytes 524288 | tf_op jit(solution)/shard_map/all_to_all | solution.py:247
  56.8 0.0 copy-start.2
  56.8 3.4 %update.1 = f32[8,2,256,256]{3,2,1,0:T(8,128)} custom-call(f32[1,2]{1,0:T(1,128)S(1)} %bitcast.12, f32[8,512]{1,0:T(8,128)S(1)} %get-tuple-element.12.keys_ref, f32[8,512]{1,0:T(8,128)S(1)} %get-tuple-element.13.values_ref, f32[8,2,256,256]{3,2,1,0:T(8,128)} %state_ref.5), custom_call_target="tpu_custom_call" | custom-call | flops 4194304 | bytes 8388608 | tf_op jit(solution)/shard_map/update/pallas_call | solution.py:208
  60.2 3.1 %all-to-all-done.3.terms_ref = bf16[8,32,512]{2,1,0:T(8,128)(2,1)S(1)} async-done(((bf16[8,32,512]{2,1,0:T(8,128)(2,1)}), bf16[8,32,512]{2,1,0:T(8,128)(2,1)S(1)}, u32[]{:S(2)}, u32[]{:S(2)}) %all-to-all-start.3) | async-done | bytes 262176 | tf_op jit(solution)/shard_map/all_to_all | solution.py:247
  63.3 0.0 copy-done.2
  63.3 0.7 %finish.1 = bf16[128,512]{1,0:T(8,128)(2,1)} custom-call(bf16[128,512]{1,0:T(8,128)(2,1)S(1)} %copy-done.2, bf16[8,32,512]{2,1,0:T(8,128)(2,1)S(1)} %all-to-all-done.3.terms_ref), custom_call_target="tpu_custom_call" | custom-call | tf_op jit(solution)/shard_map/finish/pallas_call | solution.py:240
  (2 shorter events, 0.0 us)
Async XLA Ops:
  0.6 1.7 %copy-start = (bf16[512,4,512]{2,1,0:T(4,128)(2,1)S(1)}, bf16[512,4,512]{2,1,0:T(4,128)(2,1)}, u32[]{:S(2)}) copy-start(bf16[512,4,512]{2,1,0:T(4,128)(2,1)} %param.8) | copy-start | bytes 6291460
  0.6 7.0 %copy-start.1 = (f32[8,2,256,256]{3,2,1,0:T(8,128)S(1)}, f32[8,2,256,256]{3,2,1,0:T(8,128)}, u32[]{:S(2)}) copy-start(f32[8,2,256,256]{3,2,1,0:T(8,128)} %state_ref.5) | copy-start | bytes 12582916
  3.1 4.5 %collective-permute-start = (bf16[4,64,512]{2,1,0:T(8,128)(2,1)S(1)}, bf16[4,64,512]{2,1,0:T(8,128)(2,1)S(1)}, u32[]{:S(2)}, u32[]{:S(2)}) collective-permute-start(bf16[4,64,512]{2,1,0:T(8,128)(2,1)S(1)} %slice.4), channel_id=1, source_target_pairs={{0,16},{16,0},{32,48},{48,32},{64,80},{80,64},{96,112},{112,96},{1... | collective-permute-start | bytes 786440 | tf_op jit(solution)/shard_map/ppermute | solution.py:182
  6.4 1.2 %collective-permute-start.1 = (f32[64,128]{1,0:T(8,128)S(1)}, f32[64,128]{1,0:T(8,128)S(1)}, u32[]{:S(2)}, u32[]{:S(2)}) collective-permute-start(f32[64,128]{1,0:T(8,128)S(1)} %get-tuple-element.10), channel_id=1, source_target_pairs={{0,16},{16,0},{32,48},{48,32},{64,80},{80,64},{96,112},{112,96},{1... | collective-permute-start | bytes 98312 | tf_op jit(solution)/shard_map/ppermute | solution.py:181
  7.6 18.2 %copy-start.3 = (f32[2]{0:T(128)S(1)}, f32[2]{0:T(128)}, u32[]{:S(2)}) copy-start(f32[2]{0:T(128)} %param.10) | copy-start | bytes 28
  25.8 14.2 %copy-start.4 = (bf16[512,512]{1,0:T(8,128)(2,1)S(1)}, bf16[512,512]{1,0:T(8,128)(2,1)}, u32[]{:S(2)}) copy-start(bf16[512,512]{1,0:T(8,128)(2,1)} %param.9) | copy-start | bytes 1572868
  53.1 10.2 %all-to-all-start.3 = ((bf16[8,32,512]{2,1,0:T(8,128)(2,1)}), bf16[8,32,512]{2,1,0:T(8,128)(2,1)S(1)}, u32[]{:S(2)}, u32[]{:S(2)}) async-start(bf16[8,32,512]{2,1,0:T(8,128)(2,1)} %middle.1), calls=%async_computation.3 | async-start | bytes 524288 | tf_op jit(solution)/shard_map/all_to_all | solution.py:247
  56.8 6.5 %copy-start.2 = (bf16[128,512]{1,0:T(8,128)(2,1)S(1)}, bf16[128,512]{1,0:T(8,128)(2,1)}, u32[]{:S(2)}) copy-start(bf16[128,512]{1,0:T(8,128)(2,1)} %tokens_ref.1) | copy-start | bytes 393220
